TPU v7x, 128 devices: a whole 4x4x4 slice. The times are simulated.
128 devices in a mesh: rows: 64 (over z_lo, x, y, core), feat: 2 (over z_hi).
Axes of the slice: x: 4, y: 4, z: 4 (z_hi: 2, z_lo: 2; z = z_hi * 2 + z_lo), core: 2. Of those that a mesh axis runs over, the one named last changes fastest.
Arguments:
- cells: bfloat16 [1024, 64, 192], P('rows', 'feat'), may hold values from -6 to 6
- split: int32 [64], replicated, may hold values from 14 to 16, as said below
- w_qkv_feat: bfloat16 [192, 576], replicated, may hold values from -0.4375 to 0.4375
- w_out_feat: bfloat16 [192, 192], replicated, may hold values from -0.4375 to 0.4375
- w_qkv_samp: bfloat16 [192, 576], replicated, may hold values from -0.4375 to 0.4375
- w_out_samp: bfloat16 [192, 192], replicated, may hold values from -0.4375 to 0.4375
- w_up: bfloat16 [192, 768], replicated, may hold values from -0.4375 to 0.4375
- w_down: bfloat16 [768, 192], replicated, may hold values from -0.21875 to 0.21875
- cotangent: bfloat16 [1024, 64, 192], P('rows', 'feat'), may hold values from -6 to 6
Outputs:
- layer_out: bfloat16 [1024, 64, 192], P('rows', 'feat')
- grad_cells: bfloat16 [1024, 64, 192], P('rows', 'feat')
- grad_qkv_feat: float32 [192, 576], replicated
- grad_out_feat: float32 [192, 192], replicated
- grad_qkv_samp: float32 [192, 576], replicated
- grad_out_samp: float32 [192, 192], replicated
- grad_up: float32 [192, 768], replicated
- grad_down: float32 [768, 192], replicated
Inputs may be any that keep to these rules, and one draw needn't show every extreme that they name: split[i] counts the training rows among the 16 rows of block i; they come first in the block and the rest of the block are query rows.
All inputs are finite; a program needn't handle non-finite values.
Results may differ from a plain program's by a relative error of at most 0.033.
Values may be sent and summed in bfloat16 or wider, within the bound.
No kernel may reach another device: no remote copies, remote signals or barrier semaphores. Data moves between devices by JAX's collectives and lax.ppermute only.
A program may use at most 128 MiB of HBM per device.

v0:
```python
import jax
import jax.numpy as jnp
from jax import lax
from jax.experimental import pallas as pl
from jax.experimental.pallas import tpu as pltpu
from jax.sharding import Mesh, PartitionSpec as P

H = 6
D = 32
E = 192
EPS = 1e-05
SCALE = D ** -0.5
EXP2_SCALE = SCALE * 1.4426950408889634
NEG = -1e30
GELU_A = 0.7978845608028654
GELU_B = 0.044715
f32 = jnp.float32
bf16 = jnp.bfloat16
EARLY = 9 * E
LATE = 3 * E
CHUNK = 40
SHARE = 64 * CHUNK


def dot(a, b):
    return jnp.dot(a, b, preferred_element_type=f32)


def dot_nt(a, b):
    return lax.dot_general(a, b, (((1,), (1,)), ((), ())), preferred_element_type=f32)


def transposed(v):
    return jnp.transpose(v.astype(f32))


def lane_mean(v):
    return dot(v.astype(bf16), jnp.full((E, E), 1.0, bf16)) * (1.0 / E)


def norm(v):
    centered = v - lane_mean(v)
    inv_std = lax.rsqrt(lane_mean(centered * centered) + EPS)
    return centered * inv_std, inv_std


def norm_back(normed, inv_std, grad):
    return inv_std * (grad - lane_mean(grad) - normed * lane_mean(grad * normed))


def place(rows, head, extra=None):
    count = rows.shape[1]
    parts = []
    if head > 0:
        parts.append(jnp.zeros((D * head, count), bf16))
    parts.append(rows)
    if head < H - 1:
        parts.append(jnp.zeros((E - D * (head + 1), count), bf16))
    if extra is not None:
        parts.append(extra)
    return jnp.concatenate(parts, axis=0)


def split_rows(delta):
    high = (-delta).astype(bf16).astype(f32)
    low = -delta - high
    at = lax.broadcasted_iota(jnp.int32, (16, delta.shape[1]), 0)
    return jnp.where(at == 0, high, jnp.where(at == 1, low, 0.0)).astype(bf16)


def pack_tiles(q, k, v, out):
    lane = lax.broadcasted_iota(jnp.int32, (E, 128), 1)
    roll = lambda t: pltpu.roll(t, 64, 1)
    low = lane < 64
    return (
        q[:, :128],
        jnp.where(low, q[:, 128:], roll(k[:, :128])),
        jnp.where(low, roll(k[:, :128]), roll(k[:, 128:])),
        v[:, :128],
        out[:, :128],
        jnp.where(low, v[:, 128:], roll(out[:, 128:])),
    )


def unpack_tiles(tile, qkv_ref, out_ref, factor):
    for t in range(4):
        qkv_ref[:, 128 * t : 128 * (t + 1)] = tile(t) * factor
    last = tile(5) * factor
    qkv_ref[:, 512:576] = last[:, :64]
    out_ref[:, :128] = tile(4) * factor
    out_ref[:, 128:192] = pltpu.roll(last, 64, 1)[:, :64]


def pad_lanes(v):
    return jnp.concatenate([v, jnp.zeros((v.shape[0], 256 - E), v.dtype)], axis=1)


def halve(core_ref, sums_scr, keep_ref, send_ref, rows):
    core = core_ref[0]
    keep_ref[...] = sums_scr[pl.ds(pl.multiple_of(core * rows, 64), rows), :]
    send_ref[...] = sums_scr[pl.ds(pl.multiple_of((1 - core) * rows, 64), rows), :]


def row_masks():
    row = (lax.broadcasted_iota(jnp.int32, (D, 128 * H), 1) // 32) % 4
    return [row == i for i in range(4)]


def same_row(masks, full):
    halves = []
    for at in (0, 128):
        part = full[at + 96 : at + 128]
        for i in range(3):
            part = jnp.where(masks[i], full[at + 32 * i : at + 32 * (i + 1)], part)
        halves.append(part)
    return jnp.concatenate(halves, axis=0)


def spread(masks, part):
    parts = [jnp.where(mask, part[at : at + D], 0.0) for at in (0, D) for mask in masks]
    return jnp.concatenate(parts, axis=0).astype(bf16)


def grouped(cells_ref, recv_ref):
    parts = [ref[128 * p : 128 * (p + 1), :] for p in range(4) for ref in (cells_ref, recv_ref)]
    return jnp.concatenate(parts, axis=0).astype(f32)


def own_lanes(v):
    return jnp.concatenate([v[:, 256 * p : 256 * p + 128] for p in range(4)], axis=1)


def attend(cells_ref, recv_ref, wt_ref, ot_ref, keep=None):
    masks = row_masks()
    one_rows = jnp.ones((16, 256), bf16)
    na = norm(grouped(cells_ref, recv_ref))[0].astype(bf16)
    qt = own_lanes(dot_nt(wt_ref[:E], na).astype(bf16))
    keys = dot_nt(na, wt_ref[E : 2 * E]).astype(bf16)
    vt = dot_nt(wt_ref[2 * E : 3 * E], na).astype(bf16)
    if keep is not None:
        na_ref, qt_ref, kt_ref, p_ref = keep
        na_ref[...] = na
        qt_ref[...] = qt
        kt_ref[...] = dot_nt(wt_ref[E : 2 * E], na).astype(bf16)
    for p in range(4):
        cols = slice(128 * p, 128 * (p + 1))
        both = slice(256 * p, 256 * (p + 1))
        rhs = jnp.concatenate([place(qt[D * h : D * (h + 1), cols], h) for h in range(H)], axis=1)
        scores = same_row(masks, dot(keys[both], rhs))
        e = jnp.exp2((scores - jnp.max(scores, axis=0, keepdims=True)) * EXP2_SCALE)
        wide_e = spread(masks, e)
        invs = []
        for h in range(H):
            heads = slice(D * h, D * (h + 1))
            wide = slice(128 * h, 128 * (h + 1))
            out = dot(jnp.concatenate([vt[heads, both], one_rows], axis=0), wide_e[:, wide])
            inv = 1.0 / out[D : D + 1]
            invs.append(inv)
            ot_ref[heads, cols] = out[:D] * inv
        if keep is not None:
            p_ref[p] = (e * jnp.concatenate(invs, axis=1)).astype(bf16)


def row_forward(cells_ref, cot_ref, recv_ref, wt_ref, mid_ref, ot_scr):
    attend(cells_ref, recv_ref, wt_ref, ot_scr)
    mid = cells_ref[...].astype(f32) + dot(transposed(ot_scr[...]).astype(bf16), wt_ref[3 * E :])
    both = jnp.concatenate([mid, cot_ref[...].astype(f32)], axis=1).reshape(16, 32, 2 * E)
    mid_ref[...] = jnp.swapaxes(both, 0, 1).reshape(512, 2 * E).astype(bf16)


def row_again(cells_ref, recv_ref, wt_ref, ot_ref, *rest):
    keep, ot_scr = rest[:-1], rest[-1]
    attend(cells_ref, recv_ref, wt_ref, ot_scr, keep)
    ot_ref[...] = ot_scr[...].astype(bf16)


def row_backward(
    core_ref, rows_ref, wt_ref, ot_ref, na_ref, qt_ref, kt_ref, p_ref,
    lay_ref, dmid_ref, dq_ref, dk_ref, dv_ref, keep_ref, send_ref, sums_scr, dqt_scr, dk_scr, dv_scr,
):
    both = jnp.swapaxes(rows_ref[...].astype(f32).reshape(32, 16, 2 * E), 0, 1).reshape(512, 2 * E)
    lay_ref[...] = both[:, E:].astype(bf16)
    dmid_ref[...] = both[:, :E]
    dmid_low = both[:, :E].astype(bf16)
    sum_out = dot(ot_ref[...], dmid_low)
    d_att = dot_nt(wt_ref[3 * E :], dmid_low).astype(bf16)
    na = na_ref[...]
    lane = lax.broadcasted_iota(jnp.int32, (1024, 256), 1)
    ones = jnp.where((lane == E) | (lane == E + 1), 1.0, 0.0)
    va = (pad_lanes(dot_nt(na, wt_ref[2 * E : 3 * E])) + ones).astype(bf16)
    masks = row_masks()
    for p in range(4):
        cols = slice(128 * p, 128 * (p + 1))
        both = slice(256 * p, 256 * (p + 1))
        blocks = []
        for h in range(H):
            heads = slice(D * h, D * (h + 1))
            d_out = d_att[heads, cols]
            delta = jnp.sum(d_out.astype(f32) * ot_ref[heads, cols].astype(f32), axis=0, keepdims=True)
            blocks.append(place(d_out, h, split_rows(delta)))
        rhs = jnp.concatenate(blocks, axis=1)
        q_rhs = jnp.concatenate([place(qt_ref[D * h : D * (h + 1), cols], h) for h in range(H)], axis=1)
        part = p_ref[p].astype(f32)
        ds = spread(masks, part * same_row(masks, dot(va[both, : E + 16], rhs)))
        dk_scr[both, :] = dot_nt(ds, q_rhs)
        dv_scr[both, :] = dot_nt(spread(masks, part), rhs[:E])
        for h in range(H):
            heads = slice(D * h, D * (h + 1))
            dqt_scr[heads, cols] = dot(kt_ref[heads, both], ds[:, 128 * h : 128 * (h + 1)])
    dq = pad_lanes((transposed(dqt_scr[...]) * SCALE).astype(bf16))
    dk = pad_lanes((dk_scr[...] * SCALE).astype(bf16))
    dv = pad_lanes(dv_scr[...].astype(bf16))
    dq_ref[...] = dq
    dk_ref[...] = dk
    dv_ref[...] = dv
    na_t = transposed(na).astype(bf16)
    tiles = pack_tiles(dot(own_lanes(na_t), dq), dot(na_t, dk), dot(na_t, dv), pad_lanes(sum_out))
    for t in range(6):
        sums_scr[E * t : E * (t + 1), :] = tiles[t].astype(bf16)
    halve(core_ref, sums_scr, keep_ref, send_ref, LATE)


def cells_grad(dmid_ref, dq_ref, dk_ref, dv_ref, cells_ref, recv_ref, wt_ref, own_ref, other_ref):
    grad = dot(dk_ref[:, :E], wt_ref[E : 2 * E]) + dot(dv_ref[:, :E], wt_ref[2 * E : 3 * E])
    split = [jnp.concatenate([grad[256 * p + at : 256 * p + at + 128] for p in range(4)], axis=0) for at in (0, 128)]
    normed, inv_std = norm(recv_ref[...].astype(f32))
    other_ref[...] = norm_back(normed, inv_std, split[1]).astype(bf16)
    normed, inv_std = norm(cells_ref[...].astype(f32))
    own_ref[...] = dmid_ref[...] + norm_back(normed, inv_std, split[0] + dot(dq_ref[:, :E], wt_ref[:E]))


def column(
    core_ref, own_ref, sib_ref, bias_ref, wt_ref, wup_ref, wdown_ref,
    lay_ref, dmid_ref, nsib_ref, keep_ref, send_ref,
    sums_scr, ka_scr, va_scr, vt_scr, kt_scr, qt_scr, e_scr, ds_scr, qm_scr, dm_scr, ot_scr, inv_scr, dqt_scr,
):
    n = 512
    mid_own = own_ref[:, :E].astype(f32)
    normed_own, inv_own = norm(mid_own)
    normed_sib, inv_sib = norm(sib_ref[:, :E].astype(f32))
    nb_own = normed_own.astype(bf16)
    nb = jnp.concatenate([nb_own, normed_sib.astype(bf16)], axis=0)
    lane = lax.broadcasted_iota(jnp.int32, (2 * n, 256), 1)
    at = lax.broadcasted_iota(jnp.int32, (16, 256), 0)
    col = lax.broadcasted_iota(jnp.int32, (16, 256), 1)
    place_bias = jnp.where((at == 0) & (col == E), 1.0, 0.0).astype(bf16)
    bias = dot(jnp.transpose(bias_ref[...]).astype(bf16), place_bias)
    ka_scr[...] = (pad_lanes(dot_nt(nb, wt_ref[E : 2 * E])) + bias).astype(bf16)
    ones = jnp.where((lane == E) | (lane == E + 1), 1.0, 0.0)
    va_scr[...] = (pad_lanes(dot_nt(nb, wt_ref[2 * E : 3 * E])) + ones).astype(bf16)
    qt_scr[...] = dot_nt(wt_ref[:E], nb_own).astype(bf16)
    kt_scr[...] = dot_nt(wt_ref[E : 2 * E], nb).astype(bf16)
    vt_scr[...] = dot_nt(wt_ref[2 * E : 3 * E], nb).astype(bf16)
    one_rows = jnp.ones((16, 2 * n), bf16)
    at = lax.broadcasted_iota(jnp.int32, (16, n), 0)
    extra = jnp.where(at == 0, 1.0, 0.0).astype(bf16)
    head_lane = lax.broadcasted_iota(jnp.int32, (n, 256), 1) // D
    q_cells = pad_lanes(dot_nt(nb_own, wt_ref[:E]).astype(bf16))
    for h in range(H):
        qm_scr[n * h : n * (h + 1), :] = jnp.where(head_lane == h, q_cells, 0)

    def scores_of(h):
        return dot(ka_scr[:, : E + 16], place(qt_scr[D * h : D * (h + 1), :], h, extra))

    ahead = scores_of(0)
    for h in range(H):
        heads = slice(D * h, D * (h + 1))
        scores = ahead
        if h + 1 < H:
            ahead = scores_of(h + 1)
        top = jnp.max(scores, axis=0, keepdims=True)
        e = jnp.exp2((scores - top) * EXP2_SCALE).astype(bf16)
        e_scr[:, n * h : n * (h + 1)] = e
        out = dot(jnp.concatenate([vt_scr[heads, :], one_rows], axis=0), e)
        inv = 1.0 / out[D : D + 1]
        inv_scr[8 * h : 8 * (h + 1), :] = jnp.broadcast_to(inv, (8, n))
        ot_scr[heads, :] = out[:D] * inv
    att_t = ot_scr[...]
    mid_b = (mid_own + dot(transposed(att_t).astype(bf16), wt_ref[3 * E :])).astype(bf16).astype(f32)
    normed_c, inv_c = norm(mid_b)
    nc = normed_c.astype(bf16)
    cot = own_ref[:, E:]
    pre = dot(nc, wup_ref[...])
    square = pre * pre
    tanh = jnp.tanh(GELU_A * (pre + GELU_B * square * pre))
    half = 0.5 * (1.0 + tanh)
    hidden = (pre * half).astype(bf16)
    slope = half + 0.5 * pre * (1.0 - tanh * tanh) * (GELU_A * (1.0 + 3.0 * GELU_B * square))
    d_pre = (dot(cot, wdown_ref[...]) * slope).astype(bf16)
    lay_ref[...] = mid_b + dot_nt(hidden, wdown_ref[...])
    sum_up = dot(transposed(nc).astype(bf16), d_pre).astype(bf16)
    sum_down = dot(transposed(cot).astype(bf16), hidden).astype(bf16)
    for t in range(6):
        sums_scr[E * (6 + t) : E * (7 + t), :] = sum_up[:, 128 * t : 128 * (t + 1)]
        sums_scr[E * (12 + t) : E * (13 + t), :] = sum_down[:, 128 * t : 128 * (t + 1)]
    d_mid = cot.astype(f32) + norm_back(normed_c, inv_c, dot_nt(d_pre, wup_ref[...]))
    d_mid_low = d_mid.astype(bf16)
    sum_out = dot(att_t.astype(bf16), d_mid_low)
    d_att = dot_nt(wt_ref[3 * E :], d_mid_low).astype(bf16).astype(f32)
    d_low = []
    for h in range(H):
        heads = slice(D * h, D * (h + 1))
        d_low.append((d_att[heads] * inv_scr[8 * h : 8 * h + 1, :]).astype(bf16))
    d_cells = pad_lanes(transposed(jnp.concatenate(d_low, axis=0)).astype(bf16))
    for h in range(H):
        dm_scr[n * h : n * (h + 1), :] = jnp.where(head_lane == h, d_cells, 0)

    def dprobs_of(h):
        heads = slice(D * h, D * (h + 1))
        delta = jnp.sum(d_low[h].astype(f32) * ot_scr[heads, :], axis=0, keepdims=True)
        return dot(va_scr[:, : E + 16], place(d_low[h], h, split_rows(delta)))

    ahead = dprobs_of(0)
    for h in range(H):
        heads = slice(D * h, D * (h + 1))
        dprobs = ahead
        if h + 1 < H:
            ahead = dprobs_of(h + 1)
        ds = (e_scr[:, n * h : n * (h + 1)].astype(f32) * dprobs).astype(bf16)
        ds_scr[:, n * h : n * (h + 1)] = ds
        dqt_scr[heads, :] = dot(kt_scr[heads, :], ds)
    dq = pad_lanes((transposed(dqt_scr[...]) * SCALE).astype(bf16))
    dk = (dot(ds_scr[...], qm_scr[...]) * SCALE).astype(bf16)
    dv = dot(e_scr[...], dm_scr[...]).astype(bf16)
    nb_t = transposed(nb).astype(bf16)
    tiles = pack_tiles(dot(nb_t[:, :n], dq), dot(nb_t, dk), dot(nb_t, dv), pad_lanes(sum_out))
    for t in range(6):
        sums_scr[E * t : E * (t + 1), :] = tiles[t].astype(bf16)
    halve(core_ref, sums_scr, keep_ref, send_ref, EARLY)
    grad = dot(dk[:, :E], wt_ref[E : 2 * E]) + dot(dv[:, :E], wt_ref[2 * E : 3 * E])
    grad_own = grad[:n] + dot(dq[:, :E], wt_ref[:E])
    dmid_ref[...] = d_mid_low.astype(f32) + norm_back(normed_own, inv_own, grad_own)
    nsib_ref[...] = norm_back(normed_sib, inv_sib, grad[n:]).astype(bf16)


def sum_shares(parts_ref, out_ref):
    total = jnp.sum(parts_ref[...].astype(f32), axis=0).astype(bf16)
    out_ref[...] = jnp.broadcast_to(total[None], out_ref.shape)


def join(d_own_ref, n_recv_ref, lay_ref, keep_ref, recv_ref, out_ref, early_ref):
    d_mid = d_own_ref[...] + n_recv_ref[...].astype(f32)
    out_ref[...] = jnp.concatenate([d_mid, lay_ref[...]], axis=1).astype(bf16)
    early_ref[...] = (keep_ref[...].astype(f32) + recv_ref[...].astype(f32)).astype(bf16)


def merge(early_ref, keep_ref, recv_ref, out_ref):
    out_ref[:EARLY, :] = early_ref[...]
    out_ref[EARLY : EARLY + LATE, :] = (keep_ref[...].astype(f32) + recv_ref[...].astype(f32)).astype(bf16)
    out_ref[EARLY + LATE :, :] = jnp.zeros((SHARE - EARLY - LATE, 128), bf16)


def assemble(own_ref, back_ref, grad_ref):
    grad_ref[...] = (own_ref[...] + back_ref[...].astype(f32)).astype(bf16)


def finish(core_ref, own_ref, sib_ref, qkv_f_ref, out_f_ref, qkv_s_ref, out_s_ref, up_ref, down_ref, scr):
    core = core_ref[0]
    rows = EARLY + LATE
    scr[pl.ds(pl.multiple_of(core * rows, 64), rows), :] = own_ref[:rows, :]
    scr[pl.ds(pl.multiple_of((1 - core) * rows, 64), rows), :] = sib_ref[:rows, :]
    factor = 2.0 ** -8

    def early(t):
        at = E * t if t < 9 else E * t + LATE
        return scr[at : at + E, :].astype(f32)

    def late(t):
        at = EARLY + E * t if t < 3 else 2 * EARLY + E * t
        return scr[at : at + E, :].astype(f32)

    unpack_tiles(early, qkv_s_ref, out_s_ref, factor)
    unpack_tiles(late, qkv_f_ref, out_f_ref, factor)
    for t in range(6):
        up_ref[:, 128 * t : 128 * (t + 1)] = early(6 + t) * factor
        down_ref[:, 128 * t : 128 * (t + 1)] = early(12 + t) * factor


def call(kernel, outs, scratch=(), flops=0, smem=0, name=None, mib=12, in_hbm=0, out_hbm=0, sems=0):
    vmem = pl.BlockSpec(memory_space=pltpu.VMEM)
    hbm = pl.BlockSpec(memory_space=pltpu.HBM)

    def run(*args):
        in_specs = [pl.BlockSpec(memory_space=pltpu.SMEM)] * smem + [vmem] * (len(args) - smem - in_hbm) + [hbm] * in_hbm
        moved = sum(a.size * a.dtype.itemsize for a in args) if flops else 0
        return pl.pallas_call(
            kernel,
            out_shape=[jax.ShapeDtypeStruct(s, t) for s, t in outs],
            in_specs=in_specs,
            out_specs=[vmem] * (len(outs) - out_hbm) + [hbm] * out_hbm,
            scratch_shapes=[pltpu.VMEM(s, t) for s, t in scratch] + [pltpu.SemaphoreType.DMA((sems,))] * (sems > 0),
            compiler_params=pltpu.CompilerParams(vmem_limit_bytes=mib * 1024 * 1024),
            cost_estimate=pl.CostEstimate(flops=flops, bytes_accessed=moved, transcendentals=0),
            name=name,
        )(*args)

    return run


def shards(cells, split, w_qkv_feat, w_out_feat, w_qkv_samp, w_out_samp, w_up, w_down, cotangent):
    core = lax.axis_index("core")
    group = ("zhi", "chip")
    swap = [(0, 1), (1, 0)]
    wf_t = jnp.concatenate([w_qkv_feat.T, w_out_feat], axis=0)
    ws_t = jnp.concatenate([w_qkv_samp.T, w_out_samp], axis=0)
    core_arr = core.astype(jnp.int32).reshape(1)
    cells = cells.reshape(512, E)

    recv = lax.ppermute(cells, "zhi", swap)
    (mid,) = call(
        row_forward, [((512, 2 * E), bf16)], [((E, 512), f32)], flops=900_000_000, name="row_forward"
    )(cells, cotangent.reshape(512, E), recv, wf_t)

    train = jnp.arange(16, dtype=jnp.int32)[None, :] < split[:, None]
    bias = jnp.where(train, 0.0, NEG).astype(f32).reshape(32, 2, 16).transpose(1, 0, 2).reshape(2, 512)
    bias = jnp.where(core == 0, bias, bias[::-1]).reshape(1, 1024)
    bias = jnp.pad(bias, ((0, 15), (0, 0)))
    mid, bias, ws_t = lax.optimization_barrier((mid, bias, ws_t))
    own = lax.all_to_all(mid.reshape(32, 16, 2 * E), "chip", 0, 0, tiled=True).reshape(512, 2 * E)
    sib = lax.ppermute(own, "core", swap)

    lay, d_own, n_sib, early_keep, early_send = call(
        column,
        [((512, E), f32), ((512, E), f32), ((512, E), bf16), ((EARLY, 128), bf16), ((EARLY, 128), bf16)],
        [
            ((2 * EARLY, 128), bf16),
            ((1024, 256), bf16), ((1024, 256), bf16), ((E, 1024), bf16), ((E, 1024), bf16), ((E, 512), bf16),
            ((1024, H * 512), bf16), ((1024, H * 512), bf16), ((H * 512, 256), bf16), ((H * 512, 256), bf16),
            ((E, 512), f32), ((8 * H, 512), f32), ((E, 512), f32),
        ],
        flops=8_000_000_000, smem=1, name="column", mib=32,
    )(core_arr, own, sib, bias, ws_t, w_up, w_down.T)

    n_recv = lax.ppermute(n_sib, "core", swap)
    early_recv = lax.ppermute(early_send, "core", swap)
    joined, early = call(
        join, [((512, 2 * E), bf16), ((EARLY, 128), bf16)], flops=10_000_000, name="join"
    )(d_own, n_recv, lay, early_keep, early_recv)
    joined, recv = lax.optimization_barrier((joined, recv))
    rows = lax.all_to_all(joined.reshape(32, 16, 2 * E), "chip", 0, 0, tiled=True).reshape(512, 2 * E)

    saved = call(
        row_again,
        [
            ((E, 512), bf16), ((1024, E), bf16), ((E, 512), bf16), ((E, 1024), bf16), ((4, 2 * D, 768), bf16),
        ],
        [((E, 512), f32)],
        name="row_again",
    )(cells, recv, wf_t)

    layer_out, dmid, dq, dk, dv, late_keep, late_send = call(
        row_backward,
        [
            ((512, E), bf16), ((512, E), f32), ((512, 256), bf16), ((1024, 256), bf16), ((1024, 256), bf16),
            ((LATE, 128), bf16), ((LATE, 128), bf16),
        ],
        [((2 * LATE, 128), bf16), ((E, 512), f32), ((1024, E), f32), ((1024, E), f32)],
        flops=1_500_000_000, smem=1, name="row_backward",
    )(core_arr, rows, wf_t, *saved)
    late_recv = lax.ppermute(late_send, "core", swap)
    mine, other = call(
        cells_grad, [((512, E), f32), ((512, E), bf16)], flops=20_000_000_000, name="cells_grad"
    )(dmid, dq, dk, dv, cells, recv, wf_t)
    back = lax.ppermute(other, "zhi", swap)
    late_recv, mine = lax.optimization_barrier((late_recv, mine))
    (share,) = call(merge, [((SHARE, 128), bf16)], flops=100_000_000_000, name="merge")(early, late_keep, late_recv)
    parts = lax.all_to_all(share.reshape(64, CHUNK, 128), group, 0, 0, tiled=True)
    (grad_cells,) = call(assemble, [((512, E), bf16)], flops=100_000_000_000, name="assemble")(mine, back)
    parts, grad_cells = lax.optimization_barrier((parts, grad_cells))
    (total,) = call(sum_shares, [((64, CHUNK, 128), bf16)], flops=10_000_000, name="sum_shares")(parts)
    sums = lax.all_to_all(total, group, 0, 0, tiled=True).reshape(SHARE, 128)
    sums_sib = lax.ppermute(sums, "core", swap)
    g_qkv_feat, g_out_feat, g_qkv_samp, g_out_samp, g_up, g_down_t = call(
        finish,
        [((E, 576), f32), ((E, E), f32), ((E, 576), f32), ((E, E), f32), ((E, 768), f32), ((E, 768), f32)],
        [((2 * (EARLY + LATE), 128), bf16)],
        flops=10_000_000, smem=1, name="finish",
    )(core_arr, sums, sums_sib)
    return (
        layer_out.reshape(16, 32, E), grad_cells.reshape(16, 32, E),
        g_qkv_feat, g_out_feat, g_qkv_samp, g_out_samp, g_up, g_down_t.T,
    )


def solution(mesh):
    wide = Mesh(mesh.devices.reshape(32, 2, 2), ("chip", "core", "zhi"))
    cells = P(("chip", "core"), "zhi", None)
    return jax.shard_map(
        shards,
        mesh=wide,
        in_specs=(cells, P(), P(), P(), P(), P(), P(), P(), cells),
        out_specs=(cells, cells, P(), P(), P(), P(), P(), P()),
        check_vma=False,
    )
```

profile of v0, /device:TPU:1, one launch (start us, length us, event | category | flops | bytes accessed | tf_op | source)
XLA Modules:
  0.0 120.3 jit_solution(8123790638016954052)
XLA Ops:
  0.6 4.5 %collective-permute-start = (bf16[512,192]{1,0:T(8,128)(2,1)}, bf16[512,192]{1,0:T(8,128)(2,1)S(1)}, u32[]{:S(2)}, u32[]{:S(2)}) collective-permute-start(bf16[512,192]{1,0:T(8,128)(2,1)} %bitcast.26), channel_id=1, source_target_pairs={{0,1},{1,0},{2,3},{3,2},{4,5},{5,4},{6,7},{7,6},{8,9},{9,8},{10,11... | collective-permute-start | bytes 589832 | tf_op jit(solution)/shard_map/ppermute | solution.py:409
  6.4 1.1 copy.20
  9.4 1.9 %collective-permute-done.recv_ref = bf16[512,192]{1,0:T(8,128)(2,1)S(1)} collective-permute-done((bf16[512,192]{1,0:T(8,128)(2,1)}, bf16[512,192]{1,0:T(8,128)(2,1)S(1)}, u32[]{:S(2)}, u32[]{:S(2)}) %collective-permute-start) | collective-permute-done | bytes 196640 | tf_op jit(solution)/shard_map/ppermute | solution.py:409
  11.4 2.5 %row_forward.1 = bf16[512,384]{1,0:T(8,128)(2,1)S(1)} custom-call(bf16[512,192]{1,0:T(8,128)(2,1)S(1)} %bitcast.27, bf16[512,192]{1,0:T(8,128)(2,1)S(1)} %bitcast.31, bf16[512,192]{1,0:T(8,128)(2,1)S(1)} %collective-permute-done.recv_ref, bf16[768,192]{1,0:T(8,128)(2,1)S(1)} %pad_maximum_fusion.wt_ref), custom_call_target="tpu_custom_call" | custom-call | flops 900000000 | bytes 884736 | tf_op jit(solution)/shard_map/row_forward/pallas_call | solution.py:386
  13.9 15.8 %all_to_all.20 = bf16[32,16,384]{2,1,0:T(8,128)(2,1)S(1)} all-to-all(bf16[32,16,384]{2,1,0:T(8,128)(2,1)S(1)} %bitcast.25), channel_id=1, replica_groups=mesh['chip'=32,'core'=2,'zhi'=2] {'chip'}, dimensions={0} | all-to-all | bytes 786432 | tf_op jit(solution)/shard_map/all_to_all | solution.py:419
  29.7 3.1 %collective-permute-start.1 = (bf16[512,384]{1,0:T(8,128)(2,1)S(1)}, bf16[512,384]{1,0:T(8,128)(2,1)S(1)}, u32[]{:S(2)}, u32[]{:S(2)}) collective-permute-start(bf16[512,384]{1,0:T(8,128)(2,1)S(1)} %bitcast.23), channel_id=1, source_target_pairs={{0,2},{2,0},{1,3},{3,1},{4,6},{6,4},{5,7},{7,5},{8,10},{10,8},{9,1... | collective-permute-start | bytes 1179656 | tf_op jit(solution)/shard_map/ppermute | solution.py:420
  32.8 1.3 %collective-permute-done.1.sib_ref = bf16[512,384]{1,0:T(8,128)(2,1)S(1)} collective-permute-done((bf16[512,384]{1,0:T(8,128)(2,1)S(1)}, bf16[512,384]{1,0:T(8,128)(2,1)S(1)}, u32[]{:S(2)}, u32[]{:S(2)}) %collective-permute-start.1) | collective-permute-done | bytes 393248 | tf_op jit(solution)/shard_map/ppermute | solution.py:420
  34.1 16.7 %column.1 = (f32[512,192]{1,0:T(8,128)S(1)}, f32[512,192]{1,0:T(8,128)S(1)}, bf16[512,192]{1,0:T(8,128)(2,1)S(1)}, bf16[1728,128]{1,0:T(8,128)(2,1)S(1)}, bf16[1728,128]{1,0:T(8,128)(2,1)S(1)}) custom-call(s32[1]{0:T(128)} %bitcast.core_ref, bf16[512,384]{1,0:T(8,128)(2,1)S(1)} %bitcast.24, bf16[512,384]{1,0:T(8,128)(2,1)S(1)} %collective-permute-done.1.sib_ref, ...), custom_call_target="tpu_custom_call" | custom-call | flops 8000000000 | bytes 1736708 | tf_op jit(solution)/shard_map/column/pallas_call | solution.py:386
  51.4 1.7 %collective-permute-done.2.n_recv_ref = bf16[512,192]{1,0:T(8,128)(2,1)S(1)} collective-permute-done((bf16[512,192]{1,0:T(8,128)(2,1)S(1)}, bf16[512,192]{1,0:T(8,128)(2,1)S(1)}, u32[]{:S(2)}, u32[]{:S(2)}) %collective-permute-start.2) | collective-permute-done | bytes 196640 | tf_op jit(solution)/shard_map/ppermute | solution.py:434
  53.9 3.9 %all-to-all-start.1 = ((bf16[32,16,384]{2,1,0:T(8,128)(2,1)}), bf16[32,16,384]{2,1,0:T(8,128)(2,1)S(1)}, u32[]{:S(2)}, u32[]{:S(2)}) async-start(bf16[32,16,384]{2,1,0:T(8,128)(2,1)} %bitcast.9), calls=%async_computation.1 | async-start | bytes 786432 | tf_op jit(solution)/shard_map/all_to_all | solution.py:440
  57.8 2.4 %row_again.1 = (bf16[192,512]{1,0:T(8,128)(2,1)S(1)}, bf16[1024,192]{1,0:T(8,128)(2,1)S(1)}, bf16[192,512]{1,0:T(8,128)(2,1)S(1)}, bf16[192,1024]{1,0:T(8,128)(2,1)S(1)}, bf16[4,64,768]{2,1,0:T(8,128)(2,1)S(1)}) custom-call(bf16[512,192]{1,0:T(8,128)(2,1)S(1)} %bitcast.28, bf16[512,192]{1,0:T(8,128)(2,1)S(1)} %collective-permute-done.recv_ref, ...), custom_call_target="tpu_custom_call" | custom-call | tf_op jit(solution)/shard_map/row_again/pallas_call | solution.py:386
  60.3 6.6 %all-to-all-done.1 = bf16[32,16,384]{2,1,0:T(8,128)(2,1)S(1)} async-done(((bf16[32,16,384]{2,1,0:T(8,128)(2,1)}), bf16[32,16,384]{2,1,0:T(8,128)(2,1)S(1)}, u32[]{:S(2)}, u32[]{:S(2)}) %all-to-all-start.1) | async-done | bytes 393248 | tf_op jit(solution)/shard_map/all_to_all | solution.py:440
  66.9 3.4 %row_backward.1 = (bf16[512,192]{1,0:T(8,128)(2,1)}, f32[512,192]{1,0:T(8,128)S(1)}, bf16[512,256]{1,0:T(8,128)(2,1)S(1)}, bf16[1024,256]{1,0:T(8,128)(2,1)S(1)}...) custom-call(s32[1]{0:T(128)} %bitcast.core_ref, ...), custom_call_target="tpu_custom_call" | custom-call | flops 1500000000 | bytes 2260996 | tf_op jit(solution)/shard_map/row_backward/pallas_call | solution.py:386
  70.3 2.3 %collective-permute-start.4 = (bf16[576,128]{1,0:T(8,128)(2,1)S(1)}, bf16[576,128]{1,0:T(8,128)(2,1)S(1)}, u32[]{:S(2)}, u32[]{:S(2)}) collective-permute-start(bf16[576,128]{1,0:T(8,128)(2,1)S(1)} %get-tuple-element.63), channel_id=1, source_target_pairs={{0,2},{2,0},{1,3},{3,1},{4,6},{6,4},{5,7},{7,5},{8,10},{10,8},{9,1... | collective-permute-start | bytes 442376 | tf_op jit(solution)/shard_map/ppermute | solution.py:460
  72.6 1.2 %cells_grad.1 = (f32[512,192]{1,0:T(8,128)S(1)}, bf16[512,192]{1,0:T(8,128)(2,1)S(1)}) custom-call(f32[512,192]{1,0:T(8,128)S(1)} %get-tuple-element.64.dmid_ref, bf16[512,256]{1,0:T(8,128)(2,1)S(1)} %get-tuple-element.65.dq_ref, bf16[1024,256]{1,0:T(8,128)(2,1)S(1)} %get-tuple-element.66.dk_ref, bf16[1024,256]{1,0:T(8,128)(2,1)S(1)} %get-tuple-element.67.dv_ref, ...), custom_call_target="tpu_custom_call" | custom-call | flops 20000000000 | bytes 2392064 | tf_op jit(solution)/shard_map/cells_grad/pallas_call | solution.py:386
  73.8 3.4 %collective-permute-start.5 = (bf16[512,192]{1,0:T(8,128)(2,1)S(1)}, bf16[512,192]{1,0:T(8,128)(2,1)S(1)}, u32[]{:S(2)}, u32[]{:S(2)}) collective-permute-start(bf16[512,192]{1,0:T(8,128)(2,1)S(1)} %get-tuple-element.71), channel_id=1, source_target_pairs={{0,1},{1,0},{2,3},{3,2},{4,5},{5,4},{6,7},{7,6},{8,9},{9,8},{10,11... | collective-permute-start | bytes 589832 | tf_op jit(solution)/shard_map/ppermute | solution.py:464
  77.2 0.9 merge.1
  78.2 4.6 %all-to-all-start.2 = ((bf16[64,40,128]{2,1,0:T(8,128)(2,1)}), bf16[64,40,128]{2,1,0:T(8,128)(2,1)S(1)}, u32[]{:S(2)}, u32[]{:S(2)}) async-start(bf16[64,40,128]{2,1,0:T(8,128)(2,1)} %bitcast.12), calls=%async_computation.2 | async-start | bytes 1310720 | tf_op jit(solution)/shard_map/all_to_all | solution.py:467
  82.8 1.1 collective-permute-done.5.back_ref
  84.7 12.2 %all-to-all-done.2.parts_ref = bf16[64,40,128]{2,1,0:T(8,128)(2,1)S(1)} async-done(((bf16[64,40,128]{2,1,0:T(8,128)(2,1)}), bf16[64,40,128]{2,1,0:T(8,128)(2,1)S(1)}, u32[]{:S(2)}, u32[]{:S(2)}) %all-to-all-start.2) | async-done | bytes 655392 | tf_op jit(solution)/shard_map/all_to_all | solution.py:467
  97.0 16.8 %all_to_all.21 = bf16[64,40,128]{2,1,0:T(8,128)(2,1)S(1)} all-to-all(bf16[64,40,128]{2,1,0:T(8,128)(2,1)S(1)} %sum_shares.1), channel_id=1, replica_groups=mesh['chip'=32,'core'=2,'zhi'=2] {'zhi','chip'}, dimensions={0} | all-to-all | bytes 1310720 | tf_op jit(solution)/shard_map/all_to_all | solution.py:471
  113.7 3.2 %collective-permute-start.6 = (bf16[2560,128]{1,0:T(8,128)(2,1)S(1)}, bf16[2560,128]{1,0:T(8,128)(2,1)S(1)}, u32[]{:S(2)}, u32[]{:S(2)}) collective-permute-start(bf16[2560,128]{1,0:T(8,128)(2,1)S(1)} %bitcast.20), channel_id=1, source_target_pairs={{0,2},{2,0},{1,3},{3,1},{4,6},{6,4},{5,7},{7,5},{8,10},{10,8},{9,1... | collective-permute-start | bytes 1966088 | tf_op jit(solution)/shard_map/ppermute | solution.py:472
  116.9 1.7 %collective-permute-done.6.sib_ref = bf16[2560,128]{1,0:T(8,128)(2,1)S(1)} collective-permute-done((bf16[2560,128]{1,0:T(8,128)(2,1)S(1)}, bf16[2560,128]{1,0:T(8,128)(2,1)S(1)}, u32[]{:S(2)}, u32[]{:S(2)}) %collective-permute-start.6) | collective-permute-done | bytes 655392 | tf_op jit(solution)/shard_map/ppermute | solution.py:472
  118.7 1.6 %finish.1 = (f32[192,576]{1,0:T(8,128)}, f32[192,192]{1,0:T(8,128)}, f32[192,576]{1,0:T(8,128)}, f32[192,192]{1,0:T(8,128)}, f32[192,768]{1,0:T(8,128)}, /*index=5*/f32[192,768]{1,0:T(8,128)}) custom-call(s32[1]{0:T(128)} %bitcast.core_ref, bf16[2560,128]{1,0:T(8,128)(2,1)S(1)} %bitcast.21, bf16[2560,128]{1,0:T(8,128)(2,1)S(1)} %collective-permute-done.6.sib_ref), custom_call_target="tpu_custom_call" | custom-call | flops 10000000 | bytes 1310724 | tf_op jit(solution)/shard_map/finish/pallas_call | solution.py:386
  (37 shorter events, 5.5 us)
Async XLA Ops:
  0.6 10.8 %collective-permute-start = (bf16[512,192]{1,0:T(8,128)(2,1)}, bf16[512,192]{1,0:T(8,128)(2,1)S(1)}, u32[]{:S(2)}, u32[]{:S(2)}) collective-permute-start(bf16[512,192]{1,0:T(8,128)(2,1)} %bitcast.26), channel_id=1, source_target_pairs={{0,1},{1,0},{2,3},{3,2},{4,5},{5,4},{6,7},{7,6},{8,9},{9,8},{10,11... | collective-permute-start | bytes 589832 | tf_op jit(solution)/shard_map/ppermute | solution.py:409
  5.1 0.7 copy-start.7
  6.4 1.2 copy-start.4
  7.6 0.9 copy-start.5
  8.5 0.9 copy-start.6
  9.4 2.0 %copy-start = (bf16[16,32,192]{2,1,0:T(8,128)(2,1)S(1)}, bf16[16,32,192]{2,1,0:T(8,128)(2,1)}, u32[]{:S(2)}) copy-start(bf16[16,32,192]{2,1,0:T(8,128)(2,1)} %param.9) | copy-start | bytes 589828
  9.4 2.0 %copy-start.3 = (bf16[16,32,192]{2,1,0:T(8,128)(2,1)S(1)}, bf16[16,32,192]{2,1,0:T(8,128)(2,1)}, u32[]{:S(2)}) copy-start(bf16[16,32,192]{2,1,0:T(8,128)(2,1)} %param.17) | copy-start | bytes 589828
  13.8 20.3 %copy-start.1 = (bf16[192,768]{1,0:T(8,128)(2,1)S(1)}, bf16[192,768]{1,0:T(8,128)(2,1)}, u32[]{:S(2)}) copy-start(bf16[192,768]{1,0:T(8,128)(2,1)} %wup_ref.1) | copy-start | bytes 884740
  13.9 20.2 %copy-start.2 = (bf16[768,192]{0,1:T(8,128)(2,1)S(1)}, bf16[768,192]{0,1:T(8,128)(2,1)}, u32[]{:S(2)}) copy-start(bf16[768,192]{0,1:T(8,128)(2,1)} %param.16) | copy-start | bytes 884740
  29.7 4.4 %collective-permute-start.1 = (bf16[512,384]{1,0:T(8,128)(2,1)S(1)}, bf16[512,384]{1,0:T(8,128)(2,1)S(1)}, u32[]{:S(2)}, u32[]{:S(2)}) collective-permute-start(bf16[512,384]{1,0:T(8,128)(2,1)S(1)} %bitcast.23), channel_id=1, source_target_pairs={{0,2},{2,0},{1,3},{3,1},{4,6},{6,4},{5,7},{7,5},{8,10},{10,8},{9,1... | collective-permute-start | bytes 1179656 | tf_op jit(solution)/shard_map/ppermute | solution.py:420
  50.8 2.3 %collective-permute-start.3 = (bf16[1728,128]{1,0:T(8,128)(2,1)S(1)}, bf16[1728,128]{1,0:T(8,128)(2,1)S(1)}, u32[]{:S(2)}, u32[]{:S(2)}) collective-permute-start(bf16[1728,128]{1,0:T(8,128)(2,1)S(1)} %get-tuple-element.51), channel_id=1, source_target_pairs={{0,2},{2,0},{1,3},{3,1},{4,6},{6,4},{5,7},{7,5},{8,10},{10,8},{9,1... | collective-permute-start | bytes 1327112 | tf_op jit(solution)/shard_map/ppermute | solution.py:435
  51.2 1.8 %collective-permute-start.2 = (bf16[512,192]{1,0:T(8,128)(2,1)S(1)}, bf16[512,192]{1,0:T(8,128)(2,1)S(1)}, u32[]{:S(2)}, u32[]{:S(2)}) collective-permute-start(bf16[512,192]{1,0:T(8,128)(2,1)S(1)} %get-tuple-element.48), channel_id=1, source_target_pairs={{0,2},{2,0},{1,3},{3,1},{4,6},{6,4},{5,7},{7,5},{8,10},{10,8},{9,1... | collective-permute-start | bytes 589832 | tf_op jit(solution)/shard_map/ppermute | solution.py:434
  53.9 13.0 %all-to-all-start.1 = ((bf16[32,16,384]{2,1,0:T(8,128)(2,1)}), bf16[32,16,384]{2,1,0:T(8,128)(2,1)S(1)}, u32[]{:S(2)}, u32[]{:S(2)}) async-start(bf16[32,16,384]{2,1,0:T(8,128)(2,1)} %bitcast.9), calls=%async_computation.1 | async-start | bytes 786432 | tf_op jit(solution)/shard_map/all_to_all | solution.py:440
  70.3 6.9 %collective-permute-start.4 = (bf16[576,128]{1,0:T(8,128)(2,1)S(1)}, bf16[576,128]{1,0:T(8,128)(2,1)S(1)}, u32[]{:S(2)}, u32[]{:S(2)}) collective-permute-start(bf16[576,128]{1,0:T(8,128)(2,1)S(1)} %get-tuple-element.63), channel_id=1, source_target_pairs={{0,2},{2,0},{1,3},{3,1},{4,6},{6,4},{5,7},{7,5},{8,10},{10,8},{9,1... | collective-permute-start | bytes 442376 | tf_op jit(solution)/shard_map/ppermute | solution.py:460
  73.8 10.1 %collective-permute-start.5 = (bf16[512,192]{1,0:T(8,128)(2,1)S(1)}, bf16[512,192]{1,0:T(8,128)(2,1)S(1)}, u32[]{:S(2)}, u32[]{:S(2)}) collective-permute-start(bf16[512,192]{1,0:T(8,128)(2,1)S(1)} %get-tuple-element.71), channel_id=1, source_target_pairs={{0,1},{1,0},{2,3},{3,2},{4,5},{5,4},{6,7},{7,6},{8,9},{9,8},{10,11... | collective-permute-start | bytes 589832 | tf_op jit(solution)/shard_map/ppermute | solution.py:464
  78.2 18.7 %all-to-all-start.2 = ((bf16[64,40,128]{2,1,0:T(8,128)(2,1)}), bf16[64,40,128]{2,1,0:T(8,128)(2,1)S(1)}, u32[]{:S(2)}, u32[]{:S(2)}) async-start(bf16[64,40,128]{2,1,0:T(8,128)(2,1)} %bitcast.12), calls=%async_computation.2 | async-start | bytes 1310720 | tf_op jit(solution)/shard_map/all_to_all | solution.py:467
  113.7 4.9 %collective-permute-start.6 = (bf16[2560,128]{1,0:T(8,128)(2,1)S(1)}, bf16[2560,128]{1,0:T(8,128)(2,1)S(1)}, u32[]{:S(2)}, u32[]{:S(2)}) collective-permute-start(bf16[2560,128]{1,0:T(8,128)(2,1)S(1)} %bitcast.20), channel_id=1, source_target_pairs={{0,2},{2,0},{1,3},{3,1},{4,6},{6,4},{5,7},{7,5},{8,10},{10,8},{9,1... | collective-permute-start | bytes 1966088 | tf_op jit(solution)/shard_map/ppermute | solution.py:472
where the time goes:
time: 121 us; the launch traced here: 120 us
  blocking collectives  32.6 us (27%)
  Pallas kernels  30.6 us (25%)
  waiting for transfers between devices  26.6 us (22%)
  starting transfers between devices  25.5 us (21%)
  local copies, waits for them, and re-layouts  4.1 us (3%)
    pallas_call x10, Pallas kernels, run(): pl.pallas_call(kernel, out_shape=[jax.ShapeDtypeStruct(s, t) for s, t in...  30.6 us
    all_to_all x1, blocking collectives, shards(): sums = lax.all_to_all(total, group, 0, 0, tiled=True).reshape(SHARE, 128)  16.8 us
    all_to_all x1, blocking collectives, shards(): lax.all_to_all(mid.reshape(32, 16, 2 * E), 'chip', 0, 0, tiled=True)  15.8 us
    all_to_all x1, waiting for transfers between devices, shards(): lax.all_to_all(share.reshape(64, CHUNK, 128), group, 0, 0, tiled=True)  12.2 us
    all_to_all x1, waiting for transfers between devices, shards(): lax.all_to_all(joined.reshape(32, 16, 2 * E), 'chip', 0, 0, tiled=True)  6.62 us
    all_to_all x1, starting transfers between devices, shards(): lax.all_to_all(share.reshape(64, CHUNK, 128), group, 0, 0, tiled=True)  4.64 us
    ppermute x1, starting transfers between devices, shards(): recv = lax.ppermute(cells, 'zhi', swap)  4.51 us
    all_to_all x1, starting transfers between devices, shards(): lax.all_to_all(joined.reshape(32, 16, 2 * E), 'chip', 0, 0, tiled=True)  3.88 us
  transfers between devices with their start and end apart: 9, of which 7 were waited for; matrix products, arithmetic and copies ran while one was open for 2% of the time, Pallas kernels for 4%

commit v1 on v0

--- a/solution.py
+++ b/solution.py
@@ -31,7 +31,7 @@
 
 
 def transposed(v):
-    return jnp.transpose(v.astype(f32))
+    return jnp.transpose(v)
 
 
 def lane_mean(v):
@@ -182,7 +182,6 @@
     lay_ref[...] = both[:, E:].astype(bf16)
     dmid_ref[...] = both[:, :E]
     dmid_low = both[:, :E].astype(bf16)
-    sum_out = dot(ot_ref[...], dmid_low)
     d_att = dot_nt(wt_ref[3 * E :], dmid_low).astype(bf16)
     na = na_ref[...]
     lane = lax.broadcasted_iota(jnp.int32, (1024, 256), 1)
@@ -200,6 +199,10 @@
             blocks.append(place(d_out, h, split_rows(delta)))
         rhs = jnp.concatenate(blocks, axis=1)
         q_rhs = jnp.concatenate([place(qt_ref[D * h : D * (h + 1), cols], h) for h in range(H)], axis=1)
+        if p == 0:
+            na_t = transposed(na).astype(bf16)
+        if p == 2:
+            sum_out = dot(ot_ref[...], dmid_low)
         part = p_ref[p].astype(f32)
         ds = spread(masks, part * same_row(masks, dot(va[both, : E + 16], rhs)))
         dk_scr[both, :] = dot_nt(ds, q_rhs)
@@ -213,7 +216,6 @@
     dq_ref[...] = dq
     dk_ref[...] = dk
     dv_ref[...] = dv
-    na_t = transposed(na).astype(bf16)
     tiles = pack_tiles(dot(own_lanes(na_t), dq), dot(na_t, dk), dot(na_t, dv), pad_lanes(sum_out))
     for t in range(6):
         sums_scr[E * t : E * (t + 1), :] = tiles[t].astype(bf16)
@@ -246,18 +248,12 @@
     place_bias = jnp.where((at == 0) & (col == E), 1.0, 0.0).astype(bf16)
     bias = dot(jnp.transpose(bias_ref[...]).astype(bf16), place_bias)
     ka_scr[...] = (pad_lanes(dot_nt(nb, wt_ref[E : 2 * E])) + bias).astype(bf16)
-    ones = jnp.where((lane == E) | (lane == E + 1), 1.0, 0.0)
-    va_scr[...] = (pad_lanes(dot_nt(nb, wt_ref[2 * E : 3 * E])) + ones).astype(bf16)
     qt_scr[...] = dot_nt(wt_ref[:E], nb_own).astype(bf16)
-    kt_scr[...] = dot_nt(wt_ref[E : 2 * E], nb).astype(bf16)
     vt_scr[...] = dot_nt(wt_ref[2 * E : 3 * E], nb).astype(bf16)
     one_rows = jnp.ones((16, 2 * n), bf16)
     at = lax.broadcasted_iota(jnp.int32, (16, n), 0)
     extra = jnp.where(at == 0, 1.0, 0.0).astype(bf16)
     head_lane = lax.broadcasted_iota(jnp.int32, (n, 256), 1) // D
-    q_cells = pad_lanes(dot_nt(nb_own, wt_ref[:E]).astype(bf16))
-    for h in range(H):
-        qm_scr[n * h : n * (h + 1), :] = jnp.where(head_lane == h, q_cells, 0)
 
     def scores_of(h):
         return dot(ka_scr[:, : E + 16], place(qt_scr[D * h : D * (h + 1), :], h, extra))
@@ -268,6 +264,20 @@
         scores = ahead
         if h + 1 < H:
             ahead = scores_of(h + 1)
+        if h == 0:
+            kt_scr[...] = dot_nt(wt_ref[E : 2 * E], nb).astype(bf16)
+        if h == 3:
+            ones = jnp.where((lane == E) | (lane == E + 1), 1.0, 0.0)
+            va_scr[...] = (pad_lanes(dot_nt(nb, wt_ref[2 * E : 3 * E])) + ones).astype(bf16)
+        if h == 4:
+            q_cells = pad_lanes(dot_nt(nb_own, wt_ref[:E]).astype(bf16))
+            for i in range(H):
+                qm_scr[n * i : n * (i + 1), :] = jnp.where(head_lane == i, q_cells, 0)
+        if h == 2:
+            d_hidden = dot(own_ref[:, E:], wdown_ref[...])
+        if h == 1:
+            nb_t = transposed(nb).astype(bf16)
+            cot_t = transposed(own_ref[:, E:]).astype(bf16)
         top = jnp.max(scores, axis=0, keepdims=True)
         e = jnp.exp2((scores - top) * EXP2_SCALE).astype(bf16)
         e_scr[:, n * h : n * (h + 1)] = e
@@ -282,28 +292,19 @@
     cot = own_ref[:, E:]
     pre = dot(nc, wup_ref[...])
     square = pre * pre
-    tanh = jnp.tanh(GELU_A * (pre + GELU_B * square * pre))
-    half = 0.5 * (1.0 + tanh)
-    hidden = (pre * half).astype(bf16)
-    slope = half + 0.5 * pre * (1.0 - tanh * tanh) * (GELU_A * (1.0 + 3.0 * GELU_B * square))
-    d_pre = (dot(cot, wdown_ref[...]) * slope).astype(bf16)
+    half = 0.5 * jnp.tanh(pre * (GELU_A * GELU_B * square + GELU_A)) + 0.5
+    smooth = pre * half
+    hidden = smooth.astype(bf16)
+    slope = half + (smooth - smooth * half) * (6.0 * GELU_A * GELU_B * square + 2.0 * GELU_A)
+    d_pre = (d_hidden * slope).astype(bf16)
     lay_ref[...] = mid_b + dot_nt(hidden, wdown_ref[...])
-    sum_up = dot(transposed(nc).astype(bf16), d_pre).astype(bf16)
-    sum_down = dot(transposed(cot).astype(bf16), hidden).astype(bf16)
-    for t in range(6):
-        sums_scr[E * (6 + t) : E * (7 + t), :] = sum_up[:, 128 * t : 128 * (t + 1)]
-        sums_scr[E * (12 + t) : E * (13 + t), :] = sum_down[:, 128 * t : 128 * (t + 1)]
     d_mid = cot.astype(f32) + norm_back(normed_c, inv_c, dot_nt(d_pre, wup_ref[...]))
     d_mid_low = d_mid.astype(bf16)
-    sum_out = dot(att_t.astype(bf16), d_mid_low)
     d_att = dot_nt(wt_ref[3 * E :], d_mid_low).astype(bf16).astype(f32)
     d_low = []
     for h in range(H):
         heads = slice(D * h, D * (h + 1))
         d_low.append((d_att[heads] * inv_scr[8 * h : 8 * h + 1, :]).astype(bf16))
-    d_cells = pad_lanes(transposed(jnp.concatenate(d_low, axis=0)).astype(bf16))
-    for h in range(H):
-        dm_scr[n * h : n * (h + 1), :] = jnp.where(head_lane == h, d_cells, 0)
 
     def dprobs_of(h):
         heads = slice(D * h, D * (h + 1))
@@ -316,13 +317,26 @@
         dprobs = ahead
         if h + 1 < H:
             ahead = dprobs_of(h + 1)
+        if h == 2:
+            d_cells = pad_lanes(transposed(jnp.concatenate(d_low, axis=0)).astype(bf16))
+            for i in range(H):
+                dm_scr[n * i : n * (i + 1), :] = jnp.where(head_lane == i, d_cells, 0)
+        if h == 4:
+            sum_out = dot(att_t.astype(bf16), d_mid_low)
+        if h == 1:
+            nc_t = transposed(nc).astype(bf16)
+        if h == 3:
+            sum_up = dot(nc_t, d_pre).astype(bf16)
+            sum_down = dot(cot_t, hidden).astype(bf16)
+            for t in range(6):
+                sums_scr[E * (6 + t) : E * (7 + t), :] = sum_up[:, 128 * t : 128 * (t + 1)]
+                sums_scr[E * (12 + t) : E * (13 + t), :] = sum_down[:, 128 * t : 128 * (t + 1)]
         ds = (e_scr[:, n * h : n * (h + 1)].astype(f32) * dprobs).astype(bf16)
         ds_scr[:, n * h : n * (h + 1)] = ds
         dqt_scr[heads, :] = dot(kt_scr[heads, :], ds)
     dq = pad_lanes((transposed(dqt_scr[...]) * SCALE).astype(bf16))
     dk = (dot(ds_scr[...], qm_scr[...]) * SCALE).astype(bf16)
     dv = dot(e_scr[...], dm_scr[...]).astype(bf16)
-    nb_t = transposed(nb).astype(bf16)
     tiles = pack_tiles(dot(nb_t[:, :n], dq), dot(nb_t, dk), dot(nb_t, dv), pad_lanes(sum_out))
     for t in range(6):
         sums_scr[E * t : E * (t + 1), :] = tiles[t].astype(bf16)

time: 121 us -> 119 us (0.983)
  Pallas kernels: 30.6 us -> 29.2 us
    pallas_call x10, Pallas kernels: 30.6 us -> 29.2 us  [run(): pl.pallas_call(kernel, out_shape=[jax.ShapeDtypeStruct(s, t) for s, t in...]
  transfers between devices with their start and end apart: 9 -> 9, of which waited for: 7 -> 7; matrix products, arithmetic and copies ran while one was open for 2% -> 2% of each run, Pallas kernels for 4% -> 5%
where the time goes in v1:
time: 119 us
  blocking collectives  32.6 us (27%)
  Pallas kernels  29.2 us (25%)
  waiting for transfers between devices  26.6 us (22%)
  starting transfers between devices  25.5 us (21%)
  local copies, waits for them, and re-layouts  4.1 us (3%)
    pallas_call x10, Pallas kernels, run(): pl.pallas_call(kernel, out_shape=[jax.ShapeDtypeStruct(s, t) for s, t in...  29.2 us
    all_to_all x1, blocking collectives, shards(): sums = lax.all_to_all(total, group, 0, 0, tiled=True).reshape(SHARE, 128)  16.8 us
    all_to_all x1, blocking collectives, shards(): lax.all_to_all(mid.reshape(32, 16, 2 * E), 'chip', 0, 0, tiled=True)  15.8 us
    all_to_all x1, waiting for transfers between devices, shards(): lax.all_to_all(share.reshape(64, CHUNK, 128), group, 0, 0, tiled=True)  12.2 us
    all_to_all x1, waiting for transfers between devices, shards(): lax.all_to_all(joined.reshape(32, 16, 2 * E), 'chip', 0, 0, tiled=True)  6.64 us
    all_to_all x1, starting transfers between devices, shards(): lax.all_to_all(share.reshape(64, CHUNK, 128), group, 0, 0, tiled=True)  4.64 us
    ppermute x1, starting transfers between devices, shards(): recv = lax.ppermute(cells, 'zhi', swap)  4.51 us
    all_to_all x1, starting transfers between devices, shards(): lax.all_to_all(joined.reshape(32, 16, 2 * E), 'chip', 0, 0, tiled=True)  3.88 us
  transfers between devices with their start and end apart: 9, of which 7 were waited for; matrix products, arithmetic and copies ran while one was open for 2% of the time, Pallas kernels for 5%

profile of v1, /device:TPU:1, one launch (start us, length us, event | category | flops | bytes accessed | tf_op | source)
XLA Modules:
  0.0 118.9 jit_solution(6667595954555834489)
XLA Ops:
  0.6 4.5 %collective-permute-start = (bf16[512,192]{1,0:T(8,128)(2,1)}, bf16[512,192]{1,0:T(8,128)(2,1)S(1)}, u32[]{:S(2)}, u32[]{:S(2)}) collective-permute-start(bf16[512,192]{1,0:T(8,128)(2,1)} %bitcast.26), channel_id=1, source_target_pairs={{0,1},{1,0},{2,3},{3,2},{4,5},{5,4},{6,7},{7,6},{8,9},{9,8},{10,11... | collective-permute-start | bytes 589832 | tf_op jit(solution)/shard_map/ppermute | solution.py:423
  6.4 1.1 copy.20
  9.4 1.9 %collective-permute-done.recv_ref = bf16[512,192]{1,0:T(8,128)(2,1)S(1)} collective-permute-done((bf16[512,192]{1,0:T(8,128)(2,1)}, bf16[512,192]{1,0:T(8,128)(2,1)S(1)}, u32[]{:S(2)}, u32[]{:S(2)}) %collective-permute-start) | collective-permute-done | bytes 196640 | tf_op jit(solution)/shard_map/ppermute | solution.py:423
  11.4 2.5 %row_forward.1 = bf16[512,384]{1,0:T(8,128)(2,1)S(1)} custom-call(bf16[512,192]{1,0:T(8,128)(2,1)S(1)} %bitcast.27, bf16[512,192]{1,0:T(8,128)(2,1)S(1)} %bitcast.31, bf16[512,192]{1,0:T(8,128)(2,1)S(1)} %collective-permute-done.recv_ref, bf16[768,192]{1,0:T(8,128)(2,1)S(1)} %pad_maximum_fusion.wt_ref), custom_call_target="tpu_custom_call" | custom-call | flops 900000000 | bytes 884736 | tf_op jit(solution)/shard_map/row_forward/pallas_call | solution.py:400
  13.9 15.8 %all_to_all.20 = bf16[32,16,384]{2,1,0:T(8,128)(2,1)S(1)} all-to-all(bf16[32,16,384]{2,1,0:T(8,128)(2,1)S(1)} %bitcast.25), channel_id=1, replica_groups=mesh['chip'=32,'core'=2,'zhi'=2] {'chip'}, dimensions={0} | all-to-all | bytes 786432 | tf_op jit(solution)/shard_map/all_to_all | solution.py:433
  29.7 3.1 %collective-permute-start.1 = (bf16[512,384]{1,0:T(8,128)(2,1)S(1)}, bf16[512,384]{1,0:T(8,128)(2,1)S(1)}, u32[]{:S(2)}, u32[]{:S(2)}) collective-permute-start(bf16[512,384]{1,0:T(8,128)(2,1)S(1)} %bitcast.23), channel_id=1, source_target_pairs={{0,2},{2,0},{1,3},{3,1},{4,6},{6,4},{5,7},{7,5},{8,10},{10,8},{9,1... | collective-permute-start | bytes 1179656 | tf_op jit(solution)/shard_map/ppermute | solution.py:434
  32.8 1.3 %collective-permute-done.1.sib_ref = bf16[512,384]{1,0:T(8,128)(2,1)S(1)} collective-permute-done((bf16[512,384]{1,0:T(8,128)(2,1)S(1)}, bf16[512,384]{1,0:T(8,128)(2,1)S(1)}, u32[]{:S(2)}, u32[]{:S(2)}) %collective-permute-start.1) | collective-permute-done | bytes 393248 | tf_op jit(solution)/shard_map/ppermute | solution.py:434
  34.1 15.3 %column.1 = (f32[512,192]{1,0:T(8,128)S(1)}, f32[512,192]{1,0:T(8,128)S(1)}, bf16[512,192]{1,0:T(8,128)(2,1)S(1)}, bf16[1728,128]{1,0:T(8,128)(2,1)S(1)}, bf16[1728,128]{1,0:T(8,128)(2,1)S(1)}) custom-call(s32[1]{0:T(128)} %bitcast.core_ref, bf16[512,384]{1,0:T(8,128)(2,1)S(1)} %bitcast.24, bf16[512,384]{1,0:T(8,128)(2,1)S(1)} %collective-permute-done.1.sib_ref, ...), custom_call_target="tpu_custom_call" | custom-call | flops 8000000000 | bytes 1736708 | tf_op jit(solution)/shard_map/column/pallas_call | solution.py:400
  50.0 1.7 %collective-permute-done.2.n_recv_ref = bf16[512,192]{1,0:T(8,128)(2,1)S(1)} collective-permute-done((bf16[512,192]{1,0:T(8,128)(2,1)S(1)}, bf16[512,192]{1,0:T(8,128)(2,1)S(1)}, u32[]{:S(2)}, u32[]{:S(2)}) %collective-permute-start.2) | collective-permute-done | bytes 196640 | tf_op jit(solution)/shard_map/ppermute | solution.py:448
  52.6 3.9 %all-to-all-start.1 = ((bf16[32,16,384]{2,1,0:T(8,128)(2,1)}), bf16[32,16,384]{2,1,0:T(8,128)(2,1)S(1)}, u32[]{:S(2)}, u32[]{:S(2)}) async-start(bf16[32,16,384]{2,1,0:T(8,128)(2,1)} %bitcast.9), calls=%async_computation.1 | async-start | bytes 786432 | tf_op jit(solution)/shard_map/all_to_all | solution.py:454
  56.4 2.4 %row_again.1 = (bf16[192,512]{1,0:T(8,128)(2,1)S(1)}, bf16[1024,192]{1,0:T(8,128)(2,1)S(1)}, bf16[192,512]{1,0:T(8,128)(2,1)S(1)}, bf16[192,1024]{1,0:T(8,128)(2,1)S(1)}, bf16[4,64,768]{2,1,0:T(8,128)(2,1)S(1)}) custom-call(bf16[512,192]{1,0:T(8,128)(2,1)S(1)} %bitcast.28, bf16[512,192]{1,0:T(8,128)(2,1)S(1)} %collective-permute-done.recv_ref, ...), custom_call_target="tpu_custom_call" | custom-call | tf_op jit(solution)/shard_map/row_again/pallas_call | solution.py:400
  58.9 6.6 %all-to-all-done.1 = bf16[32,16,384]{2,1,0:T(8,128)(2,1)S(1)} async-done(((bf16[32,16,384]{2,1,0:T(8,128)(2,1)}), bf16[32,16,384]{2,1,0:T(8,128)(2,1)S(1)}, u32[]{:S(2)}, u32[]{:S(2)}) %all-to-all-start.1) | async-done | bytes 393248 | tf_op jit(solution)/shard_map/all_to_all | solution.py:454
  65.5 3.5 %row_backward.1 = (bf16[512,192]{1,0:T(8,128)(2,1)}, f32[512,192]{1,0:T(8,128)S(1)}, bf16[512,256]{1,0:T(8,128)(2,1)S(1)}, bf16[1024,256]{1,0:T(8,128)(2,1)S(1)}...) custom-call(s32[1]{0:T(128)} %bitcast.core_ref, ...), custom_call_target="tpu_custom_call" | custom-call | flops 1500000000 | bytes 2260996 | tf_op jit(solution)/shard_map/row_backward/pallas_call | solution.py:400
  69.0 2.2 %collective-permute-start.4 = (bf16[576,128]{1,0:T(8,128)(2,1)S(1)}, bf16[576,128]{1,0:T(8,128)(2,1)S(1)}, u32[]{:S(2)}, u32[]{:S(2)}) collective-permute-start(bf16[576,128]{1,0:T(8,128)(2,1)S(1)} %get-tuple-element.63), channel_id=1, source_target_pairs={{0,2},{2,0},{1,3},{3,1},{4,6},{6,4},{5,7},{7,5},{8,10},{10,8},{9,1... | collective-permute-start | bytes 442376 | tf_op jit(solution)/shard_map/ppermute | solution.py:474
  71.3 1.2 %cells_grad.1 = (f32[512,192]{1,0:T(8,128)S(1)}, bf16[512,192]{1,0:T(8,128)(2,1)S(1)}) custom-call(f32[512,192]{1,0:T(8,128)S(1)} %get-tuple-element.64.dmid_ref, bf16[512,256]{1,0:T(8,128)(2,1)S(1)} %get-tuple-element.65.dq_ref, bf16[1024,256]{1,0:T(8,128)(2,1)S(1)} %get-tuple-element.66.dk_ref, bf16[1024,256]{1,0:T(8,128)(2,1)S(1)} %get-tuple-element.67.dv_ref, ...), custom_call_target="tpu_custom_call" | custom-call | flops 20000000000 | bytes 2392064 | tf_op jit(solution)/shard_map/cells_grad/pallas_call | solution.py:400
  72.5 3.4 %collective-permute-start.5 = (bf16[512,192]{1,0:T(8,128)(2,1)S(1)}, bf16[512,192]{1,0:T(8,128)(2,1)S(1)}, u32[]{:S(2)}, u32[]{:S(2)}) collective-permute-start(bf16[512,192]{1,0:T(8,128)(2,1)S(1)} %get-tuple-element.71), channel_id=1, source_target_pairs={{0,1},{1,0},{2,3},{3,2},{4,5},{5,4},{6,7},{7,6},{8,9},{9,8},{10,11... | collective-permute-start | bytes 589832 | tf_op jit(solution)/shard_map/ppermute | solution.py:478
  75.9 0.9 merge.1
  76.8 4.6 %all-to-all-start.2 = ((bf16[64,40,128]{2,1,0:T(8,128)(2,1)}), bf16[64,40,128]{2,1,0:T(8,128)(2,1)S(1)}, u32[]{:S(2)}, u32[]{:S(2)}) async-start(bf16[64,40,128]{2,1,0:T(8,128)(2,1)} %bitcast.12), calls=%async_computation.2 | async-start | bytes 1310720 | tf_op jit(solution)/shard_map/all_to_all | solution.py:481
  81.5 1.1 collective-permute-done.5.back_ref
  83.3 12.2 %all-to-all-done.2.parts_ref = bf16[64,40,128]{2,1,0:T(8,128)(2,1)S(1)} async-done(((bf16[64,40,128]{2,1,0:T(8,128)(2,1)}), bf16[64,40,128]{2,1,0:T(8,128)(2,1)S(1)}, u32[]{:S(2)}, u32[]{:S(2)}) %all-to-all-start.2) | async-done | bytes 655392 | tf_op jit(solution)/shard_map/all_to_all | solution.py:481
  95.6 16.8 %all_to_all.21 = bf16[64,40,128]{2,1,0:T(8,128)(2,1)S(1)} all-to-all(bf16[64,40,128]{2,1,0:T(8,128)(2,1)S(1)} %sum_shares.1), channel_id=1, replica_groups=mesh['chip'=32,'core'=2,'zhi'=2] {'zhi','chip'}, dimensions={0} | all-to-all | bytes 1310720 | tf_op jit(solution)/shard_map/all_to_all | solution.py:485
  112.4 3.2 %collective-permute-start.6 = (bf16[2560,128]{1,0:T(8,128)(2,1)S(1)}, bf16[2560,128]{1,0:T(8,128)(2,1)S(1)}, u32[]{:S(2)}, u32[]{:S(2)}) collective-permute-start(bf16[2560,128]{1,0:T(8,128)(2,1)S(1)} %bitcast.20), channel_id=1, source_target_pairs={{0,2},{2,0},{1,3},{3,1},{4,6},{6,4},{5,7},{7,5},{8,10},{10,8},{9,1... | collective-permute-start | bytes 1966088 | tf_op jit(solution)/shard_map/ppermute | solution.py:486
  115.6 1.7 %collective-permute-done.6.sib_ref = bf16[2560,128]{1,0:T(8,128)(2,1)S(1)} collective-permute-done((bf16[2560,128]{1,0:T(8,128)(2,1)S(1)}, bf16[2560,128]{1,0:T(8,128)(2,1)S(1)}, u32[]{:S(2)}, u32[]{:S(2)}) %collective-permute-start.6) | collective-permute-done | bytes 655392 | tf_op jit(solution)/shard_map/ppermute | solution.py:486
  117.3 1.6 %finish.1 = (f32[192,576]{1,0:T(8,128)}, f32[192,192]{1,0:T(8,128)}, f32[192,576]{1,0:T(8,128)}, f32[192,192]{1,0:T(8,128)}, f32[192,768]{1,0:T(8,128)}, /*index=5*/f32[192,768]{1,0:T(8,128)}) custom-call(s32[1]{0:T(128)} %bitcast.core_ref, bf16[2560,128]{1,0:T(8,128)(2,1)S(1)} %bitcast.21, bf16[2560,128]{1,0:T(8,128)(2,1)S(1)} %collective-permute-done.6.sib_ref), custom_call_target="tpu_custom_call" | custom-call | flops 10000000 | bytes 1310724 | tf_op jit(solution)/shard_map/finish/pallas_call | solution.py:400
  (37 shorter events, 5.5 us)
Async XLA Ops:
  0.6 10.8 %collective-permute-start = (bf16[512,192]{1,0:T(8,128)(2,1)}, bf16[512,192]{1,0:T(8,128)(2,1)S(1)}, u32[]{:S(2)}, u32[]{:S(2)}) collective-permute-start(bf16[512,192]{1,0:T(8,128)(2,1)} %bitcast.26), channel_id=1, source_target_pairs={{0,1},{1,0},{2,3},{3,2},{4,5},{5,4},{6,7},{7,6},{8,9},{9,8},{10,11... | collective-permute-start | bytes 589832 | tf_op jit(solution)/shard_map/ppermute | solution.py:423
  5.1 0.7 copy-start.7
  6.4 1.2 copy-start.4
  7.6 0.9 copy-start.5
  8.5 0.9 copy-start.6
  9.4 2.0 %copy-start = (bf16[16,32,192]{2,1,0:T(8,128)(2,1)S(1)}, bf16[16,32,192]{2,1,0:T(8,128)(2,1)}, u32[]{:S(2)}) copy-start(bf16[16,32,192]{2,1,0:T(8,128)(2,1)} %param.9) | copy-start | bytes 589828
  9.4 2.0 %copy-start.3 = (bf16[16,32,192]{2,1,0:T(8,128)(2,1)S(1)}, bf16[16,32,192]{2,1,0:T(8,128)(2,1)}, u32[]{:S(2)}) copy-start(bf16[16,32,192]{2,1,0:T(8,128)(2,1)} %param.17) | copy-start | bytes 589828
  13.8 20.3 %copy-start.1 = (bf16[192,768]{1,0:T(8,128)(2,1)S(1)}, bf16[192,768]{1,0:T(8,128)(2,1)}, u32[]{:S(2)}) copy-start(bf16[192,768]{1,0:T(8,128)(2,1)} %wup_ref.1) | copy-start | bytes 884740
  13.9 20.2 %copy-start.2 = (bf16[768,192]{0,1:T(8,128)(2,1)S(1)}, bf16[768,192]{0,1:T(8,128)(2,1)}, u32[]{:S(2)}) copy-start(bf16[768,192]{0,1:T(8,128)(2,1)} %param.16) | copy-start | bytes 884740
  29.7 4.4 %collective-permute-start.1 = (bf16[512,384]{1,0:T(8,128)(2,1)S(1)}, bf16[512,384]{1,0:T(8,128)(2,1)S(1)}, u32[]{:S(2)}, u32[]{:S(2)}) collective-permute-start(bf16[512,384]{1,0:T(8,128)(2,1)S(1)} %bitcast.23), channel_id=1, source_target_pairs={{0,2},{2,0},{1,3},{3,1},{4,6},{6,4},{5,7},{7,5},{8,10},{10,8},{9,1... | collective-permute-start | bytes 1179656 | tf_op jit(solution)/shard_map/ppermute | solution.py:434
  49.4 2.3 %collective-permute-start.3 = (bf16[1728,128]{1,0:T(8,128)(2,1)S(1)}, bf16[1728,128]{1,0:T(8,128)(2,1)S(1)}, u32[]{:S(2)}, u32[]{:S(2)}) collective-permute-start(bf16[1728,128]{1,0:T(8,128)(2,1)S(1)} %get-tuple-element.51), channel_id=1, source_target_pairs={{0,2},{2,0},{1,3},{3,1},{4,6},{6,4},{5,7},{7,5},{8,10},{10,8},{9,1... | collective-permute-start | bytes 1327112 | tf_op jit(solution)/shard_map/ppermute | solution.py:449
  49.8 1.8 %collective-permute-start.2 = (bf16[512,192]{1,0:T(8,128)(2,1)S(1)}, bf16[512,192]{1,0:T(8,128)(2,1)S(1)}, u32[]{:S(2)}, u32[]{:S(2)}) collective-permute-start(bf16[512,192]{1,0:T(8,128)(2,1)S(1)} %get-tuple-element.48), channel_id=1, source_target_pairs={{0,2},{2,0},{1,3},{3,1},{4,6},{6,4},{5,7},{7,5},{8,10},{10,8},{9,1... | collective-permute-start | bytes 589832 | tf_op jit(solution)/shard_map/ppermute | solution.py:448
  52.6 13.0 %all-to-all-start.1 = ((bf16[32,16,384]{2,1,0:T(8,128)(2,1)}), bf16[32,16,384]{2,1,0:T(8,128)(2,1)S(1)}, u32[]{:S(2)}, u32[]{:S(2)}) async-start(bf16[32,16,384]{2,1,0:T(8,128)(2,1)} %bitcast.9), calls=%async_computation.1 | async-start | bytes 786432 | tf_op jit(solution)/shard_map/all_to_all | solution.py:454
  69.0 6.9 %collective-permute-start.4 = (bf16[576,128]{1,0:T(8,128)(2,1)S(1)}, bf16[576,128]{1,0:T(8,128)(2,1)S(1)}, u32[]{:S(2)}, u32[]{:S(2)}) collective-permute-start(bf16[576,128]{1,0:T(8,128)(2,1)S(1)} %get-tuple-element.63), channel_id=1, source_target_pairs={{0,2},{2,0},{1,3},{3,1},{4,6},{6,4},{5,7},{7,5},{8,10},{10,8},{9,1... | collective-permute-start | bytes 442376 | tf_op jit(solution)/shard_map/ppermute | solution.py:474
  72.5 10.1 %collective-permute-start.5 = (bf16[512,192]{1,0:T(8,128)(2,1)S(1)}, bf16[512,192]{1,0:T(8,128)(2,1)S(1)}, u32[]{:S(2)}, u32[]{:S(2)}) collective-permute-start(bf16[512,192]{1,0:T(8,128)(2,1)S(1)} %get-tuple-element.71), channel_id=1, source_target_pairs={{0,1},{1,0},{2,3},{3,2},{4,5},{5,4},{6,7},{7,6},{8,9},{9,8},{10,11... | collective-permute-start | bytes 589832 | tf_op jit(solution)/shard_map/ppermute | solution.py:478
  76.8 18.7 %all-to-all-start.2 = ((bf16[64,40,128]{2,1,0:T(8,128)(2,1)}), bf16[64,40,128]{2,1,0:T(8,128)(2,1)S(1)}, u32[]{:S(2)}, u32[]{:S(2)}) async-start(bf16[64,40,128]{2,1,0:T(8,128)(2,1)} %bitcast.12), calls=%async_computation.2 | async-start | bytes 1310720 | tf_op jit(solution)/shard_map/all_to_all | solution.py:481
  112.4 4.9 %collective-permute-start.6 = (bf16[2560,128]{1,0:T(8,128)(2,1)S(1)}, bf16[2560,128]{1,0:T(8,128)(2,1)S(1)}, u32[]{:S(2)}, u32[]{:S(2)}) collective-permute-start(bf16[2560,128]{1,0:T(8,128)(2,1)S(1)} %bitcast.20), channel_id=1, source_target_pairs={{0,2},{2,0},{1,3},{3,1},{4,6},{6,4},{5,7},{7,5},{8,10},{10,8},{9,1... | collective-permute-start | bytes 1966088 | tf_op jit(solution)/shard_map/ppermute | solution.py:486

commit v2 on v1

--- a/solution.py
+++ b/solution.py
@@ -138,9 +138,8 @@
     keys = dot_nt(na, wt_ref[E : 2 * E]).astype(bf16)
     vt = dot_nt(wt_ref[2 * E : 3 * E], na).astype(bf16)
     if keep is not None:
-        na_ref, qt_ref, kt_ref, p_ref = keep
+        na_ref, kt_ref, p_ref = keep
         na_ref[...] = na
-        qt_ref[...] = qt
         kt_ref[...] = dot_nt(wt_ref[E : 2 * E], na).astype(bf16)
     for p in range(4):
         cols = slice(128 * p, 128 * (p + 1))
@@ -175,7 +174,7 @@
 
 
 def row_backward(
-    core_ref, rows_ref, wt_ref, ot_ref, na_ref, qt_ref, kt_ref, p_ref,
+    core_ref, rows_ref, wt_ref, ot_ref, na_ref, kt_ref, p_ref,
     lay_ref, dmid_ref, dq_ref, dk_ref, dv_ref, keep_ref, send_ref, sums_scr, dqt_scr, dk_scr, dv_scr,
 ):
     both = jnp.swapaxes(rows_ref[...].astype(f32).reshape(32, 16, 2 * E), 0, 1).reshape(512, 2 * E)
@@ -184,6 +183,8 @@
     dmid_low = both[:, :E].astype(bf16)
     d_att = dot_nt(wt_ref[3 * E :], dmid_low).astype(bf16)
     na = na_ref[...]
+    own = jnp.concatenate([na[256 * p : 256 * p + 128] for p in range(4)], axis=0)
+    qt = dot_nt(wt_ref[:E], own).astype(bf16)
     lane = lax.broadcasted_iota(jnp.int32, (1024, 256), 1)
     ones = jnp.where((lane == E) | (lane == E + 1), 1.0, 0.0)
     va = (pad_lanes(dot_nt(na, wt_ref[2 * E : 3 * E])) + ones).astype(bf16)
@@ -198,7 +199,7 @@
             delta = jnp.sum(d_out.astype(f32) * ot_ref[heads, cols].astype(f32), axis=0, keepdims=True)
             blocks.append(place(d_out, h, split_rows(delta)))
         rhs = jnp.concatenate(blocks, axis=1)
-        q_rhs = jnp.concatenate([place(qt_ref[D * h : D * (h + 1), cols], h) for h in range(H)], axis=1)
+        q_rhs = jnp.concatenate([place(qt[D * h : D * (h + 1), cols], h) for h in range(H)], axis=1)
         if p == 0:
             na_t = transposed(na).astype(bf16)
         if p == 2:
@@ -321,6 +322,8 @@
             d_cells = pad_lanes(transposed(jnp.concatenate(d_low, axis=0)).astype(bf16))
             for i in range(H):
                 dm_scr[n * i : n * (i + 1), :] = jnp.where(head_lane == i, d_cells, 0)
+        if h == 5:
+            dv = dot(e_scr[...], dm_scr[...]).astype(bf16)
         if h == 4:
             sum_out = dot(att_t.astype(bf16), d_mid_low)
         if h == 1:
@@ -336,7 +339,6 @@
         dqt_scr[heads, :] = dot(kt_scr[heads, :], ds)
     dq = pad_lanes((transposed(dqt_scr[...]) * SCALE).astype(bf16))
     dk = (dot(ds_scr[...], qm_scr[...]) * SCALE).astype(bf16)
-    dv = dot(e_scr[...], dm_scr[...]).astype(bf16)
     tiles = pack_tiles(dot(nb_t[:, :n], dq), dot(nb_t, dk), dot(nb_t, dv), pad_lanes(sum_out))
     for t in range(6):
         sums_scr[E * t : E * (t + 1), :] = tiles[t].astype(bf16)
@@ -352,9 +354,12 @@
     out_ref[...] = jnp.broadcast_to(total[None], out_ref.shape)
 
 
-def join(d_own_ref, n_recv_ref, lay_ref, keep_ref, recv_ref, out_ref, early_ref):
+def join(d_own_ref, n_recv_ref, lay_ref, out_ref):
     d_mid = d_own_ref[...] + n_recv_ref[...].astype(f32)
     out_ref[...] = jnp.concatenate([d_mid, lay_ref[...]], axis=1).astype(bf16)
+
+
+def early_add(keep_ref, recv_ref, early_ref):
     early_ref[...] = (keep_ref[...].astype(f32) + recv_ref[...].astype(f32)).astype(bf16)
 
 
@@ -446,17 +451,17 @@
     )(core_arr, own, sib, bias, ws_t, w_up, w_down.T)
 
     n_recv = lax.ppermute(n_sib, "core", swap)
+    (joined,) = call(join, [((512, 2 * E), bf16)], flops=10_000_000, name="join")(d_own, n_recv, lay)
+    joined, recv, early_send = lax.optimization_barrier((joined, recv, early_send))
+    rows = lax.all_to_all(joined.reshape(32, 16, 2 * E), "chip", 0, 0, tiled=True).reshape(512, 2 * E)
+
     early_recv = lax.ppermute(early_send, "core", swap)
-    joined, early = call(
-        join, [((512, 2 * E), bf16), ((EARLY, 128), bf16)], flops=10_000_000, name="join"
-    )(d_own, n_recv, lay, early_keep, early_recv)
-    joined, recv = lax.optimization_barrier((joined, recv))
-    rows = lax.all_to_all(joined.reshape(32, 16, 2 * E), "chip", 0, 0, tiled=True).reshape(512, 2 * E)
-
+    (early,) = call(early_add, [((EARLY, 128), bf16)], name="early_add")(early_keep, early_recv)
+    early, recv = lax.optimization_barrier((early, recv))
     saved = call(
         row_again,
         [
-            ((E, 512), bf16), ((1024, E), bf16), ((E, 512), bf16), ((E, 1024), bf16), ((4, 2 * D, 768), bf16),
+            ((E, 512), bf16), ((1024, E), bf16), ((E, 1024), bf16), ((4, 2 * D, 768), bf16),
         ],
         [((E, 512), f32)],
         name="row_again",

time: 119 us -> 119 us (level)
    pallas_call x10 -> x11, Pallas kernels: 29.2 us -> 29.2 us  [run(): pl.pallas_call(kernel, out_shape=[jax.ShapeDtypeStruct(s, t) for s, t in...]
where the time goes in v2:
time: 119 us
  blocking collectives  32.6 us (27%)
  Pallas kernels  29.2 us (25%)
  waiting for transfers between devices  26.4 us (22%)
  starting transfers between devices  25.2 us (21%)
  local copies, waits for them, and re-layouts  4.1 us (3%)
    pallas_call x11, Pallas kernels, run(): pl.pallas_call(kernel, out_shape=[jax.ShapeDtypeStruct(s, t) for s, t in...  29.2 us
    all_to_all x1, blocking collectives, shards(): sums = lax.all_to_all(total, group, 0, 0, tiled=True).reshape(SHARE, 128)  16.8 us
    all_to_all x1, blocking collectives, shards(): lax.all_to_all(mid.reshape(32, 16, 2 * E), 'chip', 0, 0, tiled=True)  15.8 us
    all_to_all x1, waiting for transfers between devices, shards(): lax.all_to_all(share.reshape(64, CHUNK, 128), group, 0, 0, tiled=True)  12.1 us
    all_to_all x1, waiting for transfers between devices, shards(): lax.all_to_all(joined.reshape(32, 16, 2 * E), 'chip', 0, 0, tiled=True)  6.96 us
    all_to_all x1, starting transfers between devices, shards(): lax.all_to_all(share.reshape(64, CHUNK, 128), group, 0, 0, tiled=True)  4.64 us
    ppermute x1, starting transfers between devices, shards(): recv = lax.ppermute(cells, 'zhi', swap)  4.51 us
    all_to_all x1, starting transfers between devices, shards(): lax.all_to_all(joined.reshape(32, 16, 2 * E), 'chip', 0, 0, tiled=True)  3.88 us
  transfers between devices with their start and end apart: 9, of which 7 were waited for; matrix products, arithmetic and copies ran while one was open for 2% of the time, Pallas kernels for 5%

profile of v2, /device:TPU:1, one launch (start us, length us, event | category | flops | bytes accessed | tf_op | source)
XLA Modules:
  0.0 118.5 jit_solution(1052138576335682422)
XLA Ops:
  0.6 4.5 %collective-permute-start = (bf16[512,192]{1,0:T(8,128)(2,1)}, bf16[512,192]{1,0:T(8,128)(2,1)S(1)}, u32[]{:S(2)}, u32[]{:S(2)}) collective-permute-start(bf16[512,192]{1,0:T(8,128)(2,1)} %bitcast.26), channel_id=1, source_target_pairs={{0,1},{1,0},{2,3},{3,2},{4,5},{5,4},{6,7},{7,6},{8,9},{9,8},{10,11... | collective-permute-start | bytes 589832 | tf_op jit(solution)/shard_map/ppermute | solution.py:428
  6.4 1.1 copy.20
  9.4 1.9 %collective-permute-done.recv_ref = bf16[512,192]{1,0:T(8,128)(2,1)S(1)} collective-permute-done((bf16[512,192]{1,0:T(8,128)(2,1)}, bf16[512,192]{1,0:T(8,128)(2,1)S(1)}, u32[]{:S(2)}, u32[]{:S(2)}) %collective-permute-start) | collective-permute-done | bytes 196640 | tf_op jit(solution)/shard_map/ppermute | solution.py:428
  11.4 2.5 %row_forward.1 = bf16[512,384]{1,0:T(8,128)(2,1)S(1)} custom-call(bf16[512,192]{1,0:T(8,128)(2,1)S(1)} %bitcast.27, bf16[512,192]{1,0:T(8,128)(2,1)S(1)} %bitcast.31, bf16[512,192]{1,0:T(8,128)(2,1)S(1)} %collective-permute-done.recv_ref, bf16[768,192]{1,0:T(8,128)(2,1)S(1)} %pad_maximum_fusion.wt_ref), custom_call_target="tpu_custom_call" | custom-call | flops 900000000 | bytes 884736 | tf_op jit(solution)/shard_map/row_forward/pallas_call | solution.py:405
  13.9 15.8 %all_to_all.20 = bf16[32,16,384]{2,1,0:T(8,128)(2,1)S(1)} all-to-all(bf16[32,16,384]{2,1,0:T(8,128)(2,1)S(1)} %bitcast.25), channel_id=1, replica_groups=mesh['chip'=32,'core'=2,'zhi'=2] {'chip'}, dimensions={0} | all-to-all | bytes 786432 | tf_op jit(solution)/shard_map/all_to_all | solution.py:438
  29.7 3.1 %collective-permute-start.1 = (bf16[512,384]{1,0:T(8,128)(2,1)S(1)}, bf16[512,384]{1,0:T(8,128)(2,1)S(1)}, u32[]{:S(2)}, u32[]{:S(2)}) collective-permute-start(bf16[512,384]{1,0:T(8,128)(2,1)S(1)} %bitcast.23), channel_id=1, source_target_pairs={{0,2},{2,0},{1,3},{3,1},{4,6},{6,4},{5,7},{7,5},{8,10},{10,8},{9,1... | collective-permute-start | bytes 1179656 | tf_op jit(solution)/shard_map/ppermute | solution.py:439
  32.8 1.3 %collective-permute-done.1.sib_ref = bf16[512,384]{1,0:T(8,128)(2,1)S(1)} collective-permute-done((bf16[512,384]{1,0:T(8,128)(2,1)S(1)}, bf16[512,384]{1,0:T(8,128)(2,1)S(1)}, u32[]{:S(2)}, u32[]{:S(2)}) %collective-permute-start.1) | collective-permute-done | bytes 393248 | tf_op jit(solution)/shard_map/ppermute | solution.py:439
  34.1 15.1 %column.1 = (f32[512,192]{1,0:T(8,128)S(1)}, f32[512,192]{1,0:T(8,128)S(1)}, bf16[512,192]{1,0:T(8,128)(2,1)S(1)}, bf16[1728,128]{1,0:T(8,128)(2,1)S(1)}, bf16[1728,128]{1,0:T(8,128)(2,1)S(1)}) custom-call(s32[1]{0:T(128)} %bitcast.core_ref, bf16[512,384]{1,0:T(8,128)(2,1)S(1)} %bitcast.24, bf16[512,384]{1,0:T(8,128)(2,1)S(1)} %collective-permute-done.1.sib_ref, ...), custom_call_target="tpu_custom_call" | custom-call | flops 8000000000 | bytes 1736708 | tf_op jit(solution)/shard_map/column/pallas_call | solution.py:405
  49.7 1.2 collective-permute-done.2.n_recv_ref
  52.1 3.9 %all-to-all-start.1 = ((bf16[32,16,384]{2,1,0:T(8,128)(2,1)}), bf16[32,16,384]{2,1,0:T(8,128)(2,1)S(1)}, u32[]{:S(2)}, u32[]{:S(2)}) async-start(bf16[32,16,384]{2,1,0:T(8,128)(2,1)} %bitcast.9), calls=%async_computation.1 | async-start | bytes 786432 | tf_op jit(solution)/shard_map/all_to_all | solution.py:456
  56.2 2.4 %row_again.1 = (bf16[192,512]{1,0:T(8,128)(2,1)S(1)}, bf16[1024,192]{1,0:T(8,128)(2,1)S(1)}, bf16[192,1024]{1,0:T(8,128)(2,1)S(1)}, bf16[4,64,768]{2,1,0:T(8,128)(2,1)S(1)}) custom-call(bf16[512,192]{1,0:T(8,128)(2,1)S(1)} %bitcast.28, bf16[512,192]{1,0:T(8,128)(2,1)S(1)} %collective-permute-done.recv_ref, bf16[768,192]{1,0:T(8,128)(2,1)S(1)} %pad_maximum_fusion.wt_ref), custom_call_target="tpu_custom_call" | custom-call | tf_op jit(solution)/shard_map/row_again/pallas_call | solution.py:405
  58.6 7.0 %all-to-all-done.1 = bf16[32,16,384]{2,1,0:T(8,128)(2,1)S(1)} async-done(((bf16[32,16,384]{2,1,0:T(8,128)(2,1)}), bf16[32,16,384]{2,1,0:T(8,128)(2,1)S(1)}, u32[]{:S(2)}, u32[]{:S(2)}) %all-to-all-start.1) | async-done | bytes 393248 | tf_op jit(solution)/shard_map/all_to_all | solution.py:456
  65.6 3.5 %row_backward.1 = (bf16[512,192]{1,0:T(8,128)(2,1)}, f32[512,192]{1,0:T(8,128)S(1)}, bf16[512,256]{1,0:T(8,128)(2,1)S(1)}, bf16[1024,256]{1,0:T(8,128)(2,1)S(1)}...) custom-call(s32[1]{0:T(128)} %bitcast.core_ref, ...), custom_call_target="tpu_custom_call" | custom-call | flops 1500000000 | bytes 2064388 | tf_op jit(solution)/shard_map/row_backward/pallas_call | solution.py:405
  69.1 1.8 %collective-permute-start.4 = (bf16[576,128]{1,0:T(8,128)(2,1)S(1)}, bf16[576,128]{1,0:T(8,128)(2,1)S(1)}, u32[]{:S(2)}, u32[]{:S(2)}) collective-permute-start(bf16[576,128]{1,0:T(8,128)(2,1)S(1)} %get-tuple-element.63), channel_id=1, source_target_pairs={{0,2},{2,0},{1,3},{3,1},{4,6},{6,4},{5,7},{7,5},{8,10},{10,8},{9,1... | collective-permute-start | bytes 442376 | tf_op jit(solution)/shard_map/ppermute | solution.py:479
  70.9 1.2 %cells_grad.1 = (f32[512,192]{1,0:T(8,128)S(1)}, bf16[512,192]{1,0:T(8,128)(2,1)S(1)}) custom-call(f32[512,192]{1,0:T(8,128)S(1)} %get-tuple-element.64.dmid_ref, bf16[512,256]{1,0:T(8,128)(2,1)S(1)} %get-tuple-element.65.dq_ref, bf16[1024,256]{1,0:T(8,128)(2,1)S(1)} %get-tuple-element.66.dk_ref, bf16[1024,256]{1,0:T(8,128)(2,1)S(1)} %get-tuple-element.67.dv_ref, ...), custom_call_target="tpu_custom_call" | custom-call | flops 20000000000 | bytes 2392064 | tf_op jit(solution)/shard_map/cells_grad/pallas_call | solution.py:405
  72.1 3.4 %collective-permute-start.5 = (bf16[512,192]{1,0:T(8,128)(2,1)S(1)}, bf16[512,192]{1,0:T(8,128)(2,1)S(1)}, u32[]{:S(2)}, u32[]{:S(2)}) collective-permute-start(bf16[512,192]{1,0:T(8,128)(2,1)S(1)} %get-tuple-element.71), channel_id=1, source_target_pairs={{0,1},{1,0},{2,3},{3,2},{4,5},{5,4},{6,7},{7,6},{8,9},{9,8},{10,11... | collective-permute-start | bytes 589832 | tf_op jit(solution)/shard_map/ppermute | solution.py:483
  75.5 0.9 merge.1
  76.4 4.6 %all-to-all-start.2 = ((bf16[64,40,128]{2,1,0:T(8,128)(2,1)}), bf16[64,40,128]{2,1,0:T(8,128)(2,1)S(1)}, u32[]{:S(2)}, u32[]{:S(2)}) async-start(bf16[64,40,128]{2,1,0:T(8,128)(2,1)} %bitcast.12), calls=%async_computation.2 | async-start | bytes 1310720 | tf_op jit(solution)/shard_map/all_to_all | solution.py:486
  81.1 1.1 collective-permute-done.5.back_ref
  82.9 12.1 %all-to-all-done.2.parts_ref = bf16[64,40,128]{2,1,0:T(8,128)(2,1)S(1)} async-done(((bf16[64,40,128]{2,1,0:T(8,128)(2,1)}), bf16[64,40,128]{2,1,0:T(8,128)(2,1)S(1)}, u32[]{:S(2)}, u32[]{:S(2)}) %all-to-all-start.2) | async-done | bytes 655392 | tf_op jit(solution)/shard_map/all_to_all | solution.py:486
  95.2 16.8 %all_to_all.21 = bf16[64,40,128]{2,1,0:T(8,128)(2,1)S(1)} all-to-all(bf16[64,40,128]{2,1,0:T(8,128)(2,1)S(1)} %sum_shares.1), channel_id=1, replica_groups=mesh['chip'=32,'core'=2,'zhi'=2] {'zhi','chip'}, dimensions={0} | all-to-all | bytes 1310720 | tf_op jit(solution)/shard_map/all_to_all | solution.py:490
  112.0 3.2 %collective-permute-start.6 = (bf16[2560,128]{1,0:T(8,128)(2,1)S(1)}, bf16[2560,128]{1,0:T(8,128)(2,1)S(1)}, u32[]{:S(2)}, u32[]{:S(2)}) collective-permute-start(bf16[2560,128]{1,0:T(8,128)(2,1)S(1)} %bitcast.20), channel_id=1, source_target_pairs={{0,2},{2,0},{1,3},{3,1},{4,6},{6,4},{5,7},{7,5},{8,10},{10,8},{9,1... | collective-permute-start | bytes 1966088 | tf_op jit(solution)/shard_map/ppermute | solution.py:491
  115.2 1.7 %collective-permute-done.6.sib_ref = bf16[2560,128]{1,0:T(8,128)(2,1)S(1)} collective-permute-done((bf16[2560,128]{1,0:T(8,128)(2,1)S(1)}, bf16[2560,128]{1,0:T(8,128)(2,1)S(1)}, u32[]{:S(2)}, u32[]{:S(2)}) %collective-permute-start.6) | collective-permute-done | bytes 655392 | tf_op jit(solution)/shard_map/ppermute | solution.py:491
  116.9 1.6 %finish.1 = (f32[192,576]{1,0:T(8,128)}, f32[192,192]{1,0:T(8,128)}, f32[192,576]{1,0:T(8,128)}, f32[192,192]{1,0:T(8,128)}, f32[192,768]{1,0:T(8,128)}, /*index=5*/f32[192,768]{1,0:T(8,128)}) custom-call(s32[1]{0:T(128)} %bitcast.core_ref, bf16[2560,128]{1,0:T(8,128)(2,1)S(1)} %bitcast.21, bf16[2560,128]{1,0:T(8,128)(2,1)S(1)} %collective-permute-done.6.sib_ref), custom_call_target="tpu_custom_call" | custom-call | flops 10000000 | bytes 1310724 | tf_op jit(solution)/shard_map/finish/pallas_call | solution.py:405
  (38 shorter events, 5.8 us)
Async XLA Ops:
  0.6 10.8 %collective-permute-start = (bf16[512,192]{1,0:T(8,128)(2,1)}, bf16[512,192]{1,0:T(8,128)(2,1)S(1)}, u32[]{:S(2)}, u32[]{:S(2)}) collective-permute-start(bf16[512,192]{1,0:T(8,128)(2,1)} %bitcast.26), channel_id=1, source_target_pairs={{0,1},{1,0},{2,3},{3,2},{4,5},{5,4},{6,7},{7,6},{8,9},{9,8},{10,11... | collective-permute-start | bytes 589832 | tf_op jit(solution)/shard_map/ppermute | solution.py:428
  5.1 0.7 copy-start.7
  6.4 1.2 copy-start.4
  7.6 0.9 copy-start.5
  8.5 0.9 copy-start.6
  9.4 2.0 %copy-start = (bf16[16,32,192]{2,1,0:T(8,128)(2,1)S(1)}, bf16[16,32,192]{2,1,0:T(8,128)(2,1)}, u32[]{:S(2)}) copy-start(bf16[16,32,192]{2,1,0:T(8,128)(2,1)} %param.9) | copy-start | bytes 589828
  9.4 2.0 %copy-start.3 = (bf16[16,32,192]{2,1,0:T(8,128)(2,1)S(1)}, bf16[16,32,192]{2,1,0:T(8,128)(2,1)}, u32[]{:S(2)}) copy-start(bf16[16,32,192]{2,1,0:T(8,128)(2,1)} %param.17) | copy-start | bytes 589828
  13.8 20.3 %copy-start.1 = (bf16[192,768]{1,0:T(8,128)(2,1)S(1)}, bf16[192,768]{1,0:T(8,128)(2,1)}, u32[]{:S(2)}) copy-start(bf16[192,768]{1,0:T(8,128)(2,1)} %wup_ref.1) | copy-start | bytes 884740
  13.9 20.2 %copy-start.2 = (bf16[768,192]{0,1:T(8,128)(2,1)S(1)}, bf16[768,192]{0,1:T(8,128)(2,1)}, u32[]{:S(2)}) copy-start(bf16[768,192]{0,1:T(8,128)(2,1)} %param.16) | copy-start | bytes 884740
  29.7 4.4 %collective-permute-start.1 = (bf16[512,384]{1,0:T(8,128)(2,1)S(1)}, bf16[512,384]{1,0:T(8,128)(2,1)S(1)}, u32[]{:S(2)}, u32[]{:S(2)}) collective-permute-start(bf16[512,384]{1,0:T(8,128)(2,1)S(1)} %bitcast.23), channel_id=1, source_target_pairs={{0,2},{2,0},{1,3},{3,1},{4,6},{6,4},{5,7},{7,5},{8,10},{10,8},{9,1... | collective-permute-start | bytes 1179656 | tf_op jit(solution)/shard_map/ppermute | solution.py:439
  49.3 1.6 %collective-permute-start.2 = (bf16[512,192]{1,0:T(8,128)(2,1)S(1)}, bf16[512,192]{1,0:T(8,128)(2,1)S(1)}, u32[]{:S(2)}, u32[]{:S(2)}) collective-permute-start(bf16[512,192]{1,0:T(8,128)(2,1)S(1)} %get-tuple-element.48), channel_id=1, source_target_pairs={{0,2},{2,0},{1,3},{3,1},{4,6},{6,4},{5,7},{7,5},{8,10},{10,8},{9,1... | collective-permute-start | bytes 589832 | tf_op jit(solution)/shard_map/ppermute | solution.py:453
  51.8 4.3 %collective-permute-start.3 = (bf16[1728,128]{1,0:T(8,128)(2,1)S(1)}, bf16[1728,128]{1,0:T(8,128)(2,1)S(1)}, u32[]{:S(2)}, u32[]{:S(2)}) collective-permute-start(bf16[1728,128]{1,0:T(8,128)(2,1)S(1)} %get-tuple-element.53), channel_id=1, source_target_pairs={{0,2},{2,0},{1,3},{3,1},{4,6},{6,4},{5,7},{7,5},{8,10},{10,8},{9,1... | collective-permute-start | bytes 1327112 | tf_op jit(solution)/shard_map/ppermute | solution.py:458
  52.1 13.4 %all-to-all-start.1 = ((bf16[32,16,384]{2,1,0:T(8,128)(2,1)}), bf16[32,16,384]{2,1,0:T(8,128)(2,1)S(1)}, u32[]{:S(2)}, u32[]{:S(2)}) async-start(bf16[32,16,384]{2,1,0:T(8,128)(2,1)} %bitcast.9), calls=%async_computation.1 | async-start | bytes 786432 | tf_op jit(solution)/shard_map/all_to_all | solution.py:456
  69.1 6.4 %collective-permute-start.4 = (bf16[576,128]{1,0:T(8,128)(2,1)S(1)}, bf16[576,128]{1,0:T(8,128)(2,1)S(1)}, u32[]{:S(2)}, u32[]{:S(2)}) collective-permute-start(bf16[576,128]{1,0:T(8,128)(2,1)S(1)} %get-tuple-element.63), channel_id=1, source_target_pairs={{0,2},{2,0},{1,3},{3,1},{4,6},{6,4},{5,7},{7,5},{8,10},{10,8},{9,1... | collective-permute-start | bytes 442376 | tf_op jit(solution)/shard_map/ppermute | solution.py:479
  72.1 10.1 %collective-permute-start.5 = (bf16[512,192]{1,0:T(8,128)(2,1)S(1)}, bf16[512,192]{1,0:T(8,128)(2,1)S(1)}, u32[]{:S(2)}, u32[]{:S(2)}) collective-permute-start(bf16[512,192]{1,0:T(8,128)(2,1)S(1)} %get-tuple-element.71), channel_id=1, source_target_pairs={{0,1},{1,0},{2,3},{3,2},{4,5},{5,4},{6,7},{7,6},{8,9},{9,8},{10,11... | collective-permute-start | bytes 589832 | tf_op jit(solution)/shard_map/ppermute | solution.py:483
  76.4 18.6 %all-to-all-start.2 = ((bf16[64,40,128]{2,1,0:T(8,128)(2,1)}), bf16[64,40,128]{2,1,0:T(8,128)(2,1)S(1)}, u32[]{:S(2)}, u32[]{:S(2)}) async-start(bf16[64,40,128]{2,1,0:T(8,128)(2,1)} %bitcast.12), calls=%async_computation.2 | async-start | bytes 1310720 | tf_op jit(solution)/shard_map/all_to_all | solution.py:486
  112.0 4.9 %collective-permute-start.6 = (bf16[2560,128]{1,0:T(8,128)(2,1)S(1)}, bf16[2560,128]{1,0:T(8,128)(2,1)S(1)}, u32[]{:S(2)}, u32[]{:S(2)}) collective-permute-start(bf16[2560,128]{1,0:T(8,128)(2,1)S(1)} %bitcast.20), channel_id=1, source_target_pairs={{0,2},{2,0},{1,3},{3,1},{4,6},{6,4},{5,7},{7,5},{8,10},{10,8},{9,1... | collective-permute-start | bytes 1966088 | tf_op jit(solution)/shard_map/ppermute | solution.py:491
